TPU v7x, 128 devices: a whole 4x4x4 slice. The times are simulated.
128 devices in a mesh: gx: 32 (over y, x_hi, z), gy: 4 (over x_lo, core).
Axes of the slice: x: 4 (x_hi: 2, x_lo: 2; x = x_hi * 2 + x_lo), y: 4, z: 4, core: 2. Of those that a mesh axis runs over, the one named last changes fastest.
Arguments:
- inputs: bfloat16 [32, 128, 32, 128], P(None, 'gx', 'gy'), may hold values from -6 to 6
- diffusion: bfloat16 [128, 32, 128], P('gx', 'gy'), may hold values from 0.049804688 to 0.5
- spectral: bfloat16 [64, 16, 2, 32, 1024], P('gx', 'gy'), may hold values from -1 to 1
- pointwise: bfloat16 [32, 32], replicated, may hold values from -1 to 1
- offsets: float32 [32], replicated, may hold values from -1 to 1
Outputs:
- activated: bfloat16 [32, 128, 32, 128], P(None, 'gx', 'gy')
All inputs are finite; a program needn't handle non-finite values.
Results may differ from a plain program's by a relative error of at most 0.006.
Values may be sent and summed in bfloat16 or wider, within the bound.
A program may use at most 64 MiB of HBM per device.

v0:
```python
import math

import jax
import jax.numpy as jnp
from jax import lax
from jax.sharding import Mesh
from jax.sharding import PartitionSpec as P

C = 32
KX_DEV = 2
MY = 16
MZ = 32
CX = 4
CY = 8
NZ = 128
GX = ("gx_0", "gx_1", "gx_2")


def in_blocks(x, dim, peers):
    before, after = (x.shape[:dim], x.shape[dim + 1 :])
    return jnp.moveaxis(x.reshape(*before, peers, -1, *after), dim, 0)


def summed_on_arrival(x, axis, dim):
    peers = lax.axis_size(axis)
    parts = lax.all_to_all(in_blocks(x, dim, peers), axis, 0, 0, tiled=True)
    return jnp.sum(parts, axis=0)


def laid_out(parts, dim):
    parts = jnp.moveaxis(parts, 0, dim)
    lengths = parts.shape
    return parts.reshape(*lengths[:dim], lengths[dim] * lengths[dim + 1], *lengths[dim + 2 :])


def exchange_in_order(parts, axes, sequence):
    inside = parts.shape[1:]
    out = parts.reshape(*(lax.axis_size(a) for a in axes), *inside)
    for k in sequence:
        out = lax.all_to_all(out, axes[k], k, k, tiled=True)
    return out.reshape(-1, *inside)


def one_axis_at_a_time(x, axes, sequence, split_dim, concat_dim):
    parts = in_blocks(x, split_dim, lax.axis_size(axes))
    return laid_out(exchange_in_order(parts, axes, sequence), concat_dim)


def from_everyone(x, axis):
    copies = jnp.broadcast_to(x, (lax.axis_size(axis), *x.shape))
    return lax.all_to_all(copies, axis, split_axis=0, concat_axis=0, tiled=True)


def gathered_copies(x, axis, dim):
    return laid_out(from_everyone(x, axis), dim)


def frequencies(modes):
    indices = jnp.arange(modes, dtype=jnp.int32)
    return jnp.where(indices < modes // 2, indices, indices - modes)


def phase_table(positions, waves, length, rotate):
    windings = positions[:, None] * waves[None, :] % length
    angles = 2.0 * math.pi / length * windings.astype(jnp.float32)
    cosine = jnp.cos(angles)
    sines = rotate * jnp.sin(angles)
    from_real = jnp.stack([cosine, sines], axis=-1)
    from_imag = jnp.stack([-sines, cosine], axis=-1)
    return jnp.stack([from_real, from_imag], axis=1)


def z_tables(length_z, modes_z):
    positions = jnp.arange(length_z, dtype=jnp.int32)
    waves = jnp.arange(modes_z, dtype=jnp.int32)
    forward = phase_table(positions, waves, length_z, -1.0)[:, 0, :, :]
    forward = jnp.transpose(forward, (0, 2, 1)).reshape(length_z, 2 * modes_z)
    backward = phase_table(positions, waves, length_z, 1.0)[:, :, :, 0]
    backward = jnp.transpose(backward, (1, 2, 0)).reshape(2 * modes_z, length_z)
    return (forward.astype(jnp.bfloat16), backward)


def contract(u_part, w_part):
    return jnp.einsum("cklz,klcoz->oklz", u_part, w_part, precision=lax.Precision.HIGHEST)


def on_device(inputs, diffusion, spectral, pointwise, offsets):
    highest = lax.Precision.HIGHEST
    ranks_x = lax.axis_size(GX)
    ranks_y = lax.axis_size("gy")
    total_x = CX * ranks_x
    total_y = CY * ranks_y
    owned_x = KX_DEV
    modes_x = KX_DEV * ranks_x
    owned_y = MY // ranks_y
    lane_count = C * owned_y * MZ
    y_cells = lax.axis_index("gy") * CY + jnp.arange(CY, dtype=jnp.int32)
    all_x = jnp.arange(total_x, dtype=jnp.int32)
    z_forward, z_inverse = z_tables(NZ, MZ)
    diagonal_pair = jnp.eye(2, dtype=jnp.bfloat16)
    paired_table = (diagonal_pair[:, None, :, None] * z_forward[None, :, None, :]).reshape(
        2 * NZ, 4 * MZ
    )
    z_spectrum = jnp.dot(
        inputs.reshape(-1, 2 * NZ), paired_table, preferred_element_type=jnp.float32
    )
    z_spectrum = z_spectrum.reshape(C, CX, CY, 2, MZ)
    y_table = phase_table(y_cells, frequencies(MY), total_y, -1.0)
    y_partial = jnp.einsum("cxyqz,yqkp->cxkpz", z_spectrum, y_table, precision=highest)
    column = summed_on_arrival(y_partial.reshape(C, CX, MY * 2 * MZ), "gy", 2)
    column = column.reshape(C, CX, owned_y, 2, MZ)
    lines = jnp.transpose(column, (1, 3, 0, 2, 4)).reshape(CX, 2, lane_count)
    lines = one_axis_at_a_time(lines, GX, (0, 1, 2), 2, 0)
    full_table = phase_table(all_x, frequencies(modes_x), total_x, -1.0)
    spectra = jnp.einsum("xqs,xqap->aps", lines, full_table, precision=highest)
    blocks = lax.all_to_all(spectra, GX, split_axis=0, concat_axis=2, tiled=True)
    blocks = blocks.reshape(owned_x, 2, C, owned_y, MZ)
    owned = jnp.transpose(blocks, (2, 0, 3, 1, 4))
    owned = owned * (1.0 / math.sqrt(total_x * total_y * NZ))
    weights = spectral.astype(jnp.float32).reshape(owned_x, owned_y, 2, C, C, MZ)
    w_real = weights[:, :, 0]
    w_imag = weights[:, :, 1]
    u_real = owned[:, :, :, 0]
    u_imag = owned[:, :, :, 1]
    y_real = contract(u_real, w_real) - contract(u_imag, w_imag)
    y_imag = contract(u_real, w_imag) + contract(u_imag, w_real)
    mixed = jnp.stack([y_real, y_imag], axis=3).astype(jnp.bfloat16)
    y_inverse = jnp.transpose(phase_table(y_cells, frequencies(MY), total_y, 1.0), (2, 1, 0, 3))
    pencils = jnp.transpose(mixed, (1, 3, 0, 2, 4)).reshape(owned_x, 2, lane_count)
    pencils = lax.all_to_all(pencils, GX, split_axis=2, concat_axis=0, tiled=True)
    full_inverse = jnp.transpose(
        phase_table(all_x, frequencies(modes_x), total_x, 1.0), (2, 1, 0, 3)
    )
    cells = jnp.einsum(
        "aqs,aqxp->xps", pencils.astype(jnp.float32), full_inverse, precision=highest
    )
    cells = lax.all_to_all(
        cells.astype(jnp.bfloat16), GX, split_axis=0, concat_axis=2, tiled=True
    ).astype(cells.dtype)
    back_x = jnp.transpose(cells.reshape(CX, 2, C, owned_y, MZ), (2, 0, 3, 1, 4))
    y_lines = gathered_copies(
        back_x.reshape(C, CX, owned_y * 2 * MZ).astype(jnp.bfloat16), "gy", 2
    ).astype(jnp.float32)
    y_lines = y_lines.reshape(C, CX, MY, 2, MZ)
    spatial = jnp.einsum("cxkqz,kqyp->cxypz", y_lines, y_inverse, precision=highest)
    spectral_out = jnp.dot(
        spatial.reshape(-1, 2 * MZ),
        z_inverse,
        precision=highest,
        preferred_element_type=jnp.float32,
    )
    spectral_out = spectral_out.reshape(C, CX, CY, NZ) * (1.0 / math.sqrt(modes_x * MY * MZ))
    mixing = jnp.dot(pointwise, inputs.reshape(C, -1), preferred_element_type=jnp.float32).reshape(
        C, CX, CY, NZ
    )
    widened = inputs.astype(jnp.float32)
    padded = jnp.pad(widened, ((0, 0), (0, 0), (0, 0), (1, 1)))
    curvature = padded[:, :, :, 2:] - 2.0 * widened + padded[:, :, :, :-2]
    summed_all = (
        spectral_out
        + mixing
        + diffusion.astype(jnp.float32)[None] * curvature
        + offsets[:, None, None, None]
    )
    return jax.nn.gelu(summed_all, approximate=False).astype(jnp.bfloat16)


def solution(mesh):
    split = Mesh(mesh.devices.reshape(4, 2, 4, mesh.shape["gy"]), ("gx_0", "gx_1", "gx_2", "gy"))
    return jax.shard_map(
        on_device,
        mesh=split,
        in_specs=(
            P(None, GX, "gy", None),
            P(GX, "gy", None),
            P(GX, "gy", None, None, None),
            P(),
            P(),
        ),
        out_specs=P(None, GX, "gy", None),
        check_vma=False,
    )
```

profile of v0, /device:TPU:1, one launch (start us, length us, event | category | flops | bytes accessed | tf_op | source)
XLA Modules:
  0.0 133.2 jit_solution(18200039287444922614)
XLA Ops:
  2.7 1.8 %convolution_bitcast_fusion = f32[32,4,16,2,32]{4,2,1,0,3:T(8,128)S(1)} fusion(f32[32,4,8,2,32]{4,3,2,1,0:T(2,128)S(1)} %reshape.618, f32[8,1,16,2]{2,0,1,3:T(8,128)S(1)} %get-tuple-element.20, f32[8,1,16,2]{2,0,1,3:T(8,128)S(1)} %get-tuple-element.21), kind=kOutput, calls=%fused_computation.10 | convolution fusion | flops 25166336 | bytes 788480 | tf_op jit(solution)/shard_map/cxyqz,yqkp->cxkpz/dot_general | solution.py:109
  4.5 1.7 %copy.43 = f32[32,4,16,2,32]{4,3,2,1,0:T(2,128)S(1)} copy(f32[32,4,16,2,32]{4,2,1,0,3:T(8,128)S(1)} %convolution_bitcast_fusion) | data formatting | bytes 1048576 | tf_op jit(solution)/shard_map/cxyqz,yqkp->cxkpz/transpose | solution.py:109
  6.2 2.0 %reshape_reshape.9 = f32[32,4,4,256]{3,2,1,0:T(4,128)S(1)} reshape(f32[32,4,16,2,32]{4,3,2,1,0:T(2,128)S(1)} %copy.43) | data formatting | bytes 1048576 | tf_op jit(solution)/shard_map/reshape;reshape | solution.py:21
  8.4 12.0 %all_to_all.61 = f32[4,32,4,256]{3,2,1,0:T(4,128)S(1)} all-to-all(f32[4,32,4,256]{3,2,1,0:T(4,128)S(1)} %copy.44), channel_id=1, replica_groups=mesh['gx_0'=4,'gx_1'=2,'gx_2'=4,'gy'=4] {'gy'}, dimensions={0} | all-to-all | bytes 1048576 | tf_op jit(solution)/shard_map/all_to_all | solution.py:26
  22.1 4.2 %all-to-all-start.1 = ((f32[4,2,4,4,2,128]{5,3,2,1,4,0:T(4,128)}), f32[4,2,4,4,2,128]{5,3,2,1,4,0:T(4,128)S(1)}, u32[]{:S(2)}, u32[]{:S(2)}) async-start(f32[4,2,4,4,2,128]{5,3,2,1,4,0:T(4,128)} %copy.48), calls=%async_computation.1 | async-start | bytes 262144 | tf_op jit(solution)/shard_map/all_to_all | solution.py:40
  26.3 4.8 %all-to-all-done.1 = f32[4,2,4,4,2,128]{5,3,2,1,4,0:T(4,128)S(1)} async-done(((f32[4,2,4,4,2,128]{5,3,2,1,4,0:T(4,128)}), f32[4,2,4,4,2,128]{5,3,2,1,4,0:T(4,128)S(1)}, u32[]{:S(2)}, u32[]{:S(2)}) %all-to-all-start.1) | async-done | bytes 131104 | tf_op jit(solution)/shard_map/all_to_all | solution.py:40
  31.8 3.8 %all-to-all-start.2 = ((f32[4,2,4,4,2,128]{5,3,2,0,4,1:T(4,128)}), f32[4,2,4,4,2,128]{5,3,2,0,4,1:T(4,128)S(1)}, u32[]{:S(2)}, u32[]{:S(2)}) async-start(f32[4,2,4,4,2,128]{5,3,2,0,4,1:T(4,128)} %copy.49), calls=%async_computation.2 | async-start | bytes 262144 | tf_op jit(solution)/shard_map/all_to_all | solution.py:40
  35.9 4.4 %reshape.621 = bf16[2,4,2,32,32,32]{5,4,3,2,1,0:T(8,128)(2,1)} reshape(bf16[2,4,2,32,1024]{4,3,2,1,0:T(8,128)(2,1)S(1)} %copy-done.2) | data formatting | bytes 2097152 | tf_op jit(solution)/shard_map/reshape | solution.py:120
  41.1 5.0 %all-to-all-start.3 = ((f32[4,2,4,4,2,128]{5,3,1,0,4,2:T(4,128)}), f32[4,2,4,4,2,128]{5,3,1,0,4,2:T(4,128)S(1)}, u32[]{:S(2)}, u32[]{:S(2)}) async-start(f32[4,2,4,4,2,128]{5,3,1,0,4,2:T(4,128)} %copy.50), calls=%async_computation.3 | async-start | bytes 262144 | tf_op jit(solution)/shard_map/all_to_all | solution.py:40
  46.2 4.8 %all-to-all-done.3 = f32[4,2,4,4,2,128]{5,3,1,0,4,2:T(4,128)S(1)} async-done(((f32[4,2,4,4,2,128]{5,3,1,0,4,2:T(4,128)}), f32[4,2,4,4,2,128]{5,3,1,0,4,2:T(4,128)S(1)}, u32[]{:S(2)}, u32[]{:S(2)}) %all-to-all-start.3) | async-done | bytes 131104 | tf_op jit(solution)/shard_map/all_to_all | solution.py:40
  52.0 5.9 %all-to-all-start.4 = ((f32[64,2,128]{2,1,0:T(2,128)}), f32[64,2,128]{2,1,0:T(2,128)S(1)}, u32[]{:S(2)}, u32[]{:S(2)}) async-start(f32[64,2,128]{2,1,0:T(2,128)} %copy.52), calls=%async_computation.4 | async-start | bytes 131072 | tf_op jit(solution)/shard_map/all_to_all | solution.py:116
  58.0 8.6 %all-to-all-done.4 = f32[64,2,128]{2,1,0:T(2,128)S(1)} async-done(((f32[64,2,128]{2,1,0:T(2,128)}), f32[64,2,128]{2,1,0:T(2,128)S(1)}, u32[]{:S(2)}, u32[]{:S(2)}) %all-to-all-start.4) | async-done | bytes 65568 | tf_op jit(solution)/shard_map/all_to_all | solution.py:116
  66.9 3.6 %fusion = (f32[2,4,32,32]{2,3,1,0:T(8,128)S(1)}, f32[2,4,32,32]{2,3,1,0:T(8,128)S(1)}, f32[2,4,32,32]{2,3,1,0:T(8,128)S(1)}, f32[2,4,32,32]{2,3,1,0:T(8,128)S(1)}) fusion(f32[2,4,32,32]{2,3,1,0:T(8,128)S(1)} %copy.117, bf16[2,4,2,32,32,32]{5,4,3,2,1,0:T(8,128)(2,1)} %reshape.621, f32[2,4,32,32]{2,3,1,0:T(8,128)S(1)} %copy.118), kind=kLoop, calls=%fused_computation.4 | loop fusion | flops 2588672 | bytes 1245184
  71.0 3.6 %copy.110 = bf16[2,2,32,4,32]{1,0,4,3,2:T(2,128)(2,1)S(1)} copy(bf16[2,2,32,4,32]{4,3,2,1,0:T(4,128)(2,1)S(1)} %maximum_bitcast_fusion.2) | data formatting | bytes 65536 | tf_op jit(solution)/shard_map/reshape | solution.py:129
  74.6 4.0 %reshape.647 = bf16[32,2,256]{2,1,0:T(2,128)(2,1)} reshape(bf16[4096,2,2]{2,1,0:T(2,128)(2,1)S(1)} %bitcast.201) | data formatting | bytes 65536
  78.6 3.9 %all-to-all-start.5 = ((bf16[32,2,256]{2,1,0:T(2,128)(2,1)}), bf16[32,2,256]{2,1,0:T(2,128)(2,1)S(1)}, u32[]{:S(2)}, u32[]{:S(2)}) async-start(bf16[32,2,256]{2,1,0:T(2,128)(2,1)} %reshape.647), calls=%async_computation.5 | async-start | bytes 65536 | tf_op jit(solution)/shard_map/all_to_all | solution.py:130
  82.8 8.4 %all-to-all-done.5 = bf16[32,2,256]{2,1,0:T(2,128)(2,1)S(1)} async-done(((bf16[32,2,256]{2,1,0:T(2,128)(2,1)}), bf16[32,2,256]{2,1,0:T(2,128)(2,1)S(1)}, u32[]{:S(2)}, u32[]{:S(2)}) %all-to-all-start.5) | async-done | bytes 32800 | tf_op jit(solution)/shard_map/all_to_all | solution.py:130
  91.2 4.5 %reshape.648 = bf16[4096,2,2]{2,1,0:T(2,128)(2,1)S(1)} reshape(bf16[32,2,256]{2,1,0:T(2,128)(2,1)S(1)} %all-to-all-done.5) | data formatting | bytes 65536
  95.7 1.2 copy.111
  98.0 3.9 %all-to-all-start.6 = ((bf16[128,2,128]{2,1,0:T(2,128)(2,1)}), bf16[128,2,128]{2,1,0:T(2,128)(2,1)S(1)}, u32[]{:S(2)}, u32[]{:S(2)}) async-start(bf16[128,2,128]{2,1,0:T(2,128)(2,1)} %copy.56), calls=%async_computation.6 | async-start | bytes 131072 | tf_op jit(solution)/shard_map/all_to_all | solution.py:137
  101.8 8.8 %all-to-all-done.6 = bf16[128,2,128]{2,1,0:T(2,128)(2,1)S(1)} async-done(((bf16[128,2,128]{2,1,0:T(2,128)(2,1)}), bf16[128,2,128]{2,1,0:T(2,128)(2,1)S(1)}, u32[]{:S(2)}, u32[]{:S(2)}) %all-to-all-start.6) | async-done | bytes 65568 | tf_op jit(solution)/shard_map/all_to_all | solution.py:137
  112.2 11.5 %all-to-all-start.7 = ((bf16[4,32,4,256]{3,2,1,0:T(4,128)(2,1)}), bf16[4,32,4,256]{3,2,1,0:T(4,128)(2,1)S(1)}, u32[]{:S(2)}, u32[]{:S(2)}) async-start(bf16[4,32,4,256]{3,2,1,0:T(4,128)(2,1)} %broadcast_in_dim.2), calls=%async_computation.7 | async-start | bytes 524288 | tf_op jit(solution)/shard_map/all_to_all | solution.py:51
  123.9 4.9 %all-to-all-done.7 = bf16[4,32,4,256]{3,2,1,0:T(4,128)(2,1)S(1)} async-done(((bf16[4,32,4,256]{3,2,1,0:T(4,128)(2,1)}), bf16[4,32,4,256]{3,2,1,0:T(4,128)(2,1)S(1)}, u32[]{:S(2)}, u32[]{:S(2)}) %all-to-all-start.7) | async-done | bytes 262176 | tf_op jit(solution)/shard_map/all_to_all | solution.py:51
  130.1 3.1 %fusion.15 = bf16[32,4,8,128]{3,2,1,0:T(8,128)(2,1)} fusion(f32[32,4,8,128]{3,2,1,0:T(8,128)S(1)} %convert_element_type.170, f32[32,4,8,128]{3,0,2,1:T(8,128)S(1)} %fusion.26, f32[32,4,8,2,32]{4,2,3,1,0:T(8,128)S(1)} %convolution_bitcast_fusion.1, f32[32]{0:T(128)S(1)} %copy-done.4, f32[4,8,128]{2,1,0:T(8,128)S(1)} %convert_element_type.169, ...), kind=kOutput, calls=%fused_computation.30 | convolution fusion | flops 110239744 | bytes 1654912 | tf_op jit(solution)/shard_map/dot_general | solution.py:146
  (65 shorter events, 12.4 us)
Async XLA Ops:
  0.0 123.7 %copy-start = (bf16[32,32]{1,0:T(8,128)(2,1)S(1)}, bf16[32,32]{1,0:T(8,128)(2,1)}, u32[]{:S(2)}) copy-start(bf16[32,32]{1,0:T(8,128)(2,1)} %param.8) | copy-start | bytes 6148
  8.2 27.6 %copy-start.2 = (bf16[2,4,2,32,1024]{4,3,2,1,0:T(8,128)(2,1)S(1)}, bf16[2,4,2,32,1024]{4,3,2,1,0:T(8,128)(2,1)}, u32[]{:S(2)}) copy-start(bf16[2,4,2,32,1024]{4,3,2,1,0:T(8,128)(2,1)} %param.7) | copy-start | bytes 3145732
  22.1 9.0 %all-to-all-start.1 = ((f32[4,2,4,4,2,128]{5,3,2,1,4,0:T(4,128)}), f32[4,2,4,4,2,128]{5,3,2,1,4,0:T(4,128)S(1)}, u32[]{:S(2)}, u32[]{:S(2)}) async-start(f32[4,2,4,4,2,128]{5,3,2,1,4,0:T(4,128)} %copy.48), calls=%async_computation.1 | async-start | bytes 262144 | tf_op jit(solution)/shard_map/all_to_all | solution.py:40
  31.8 8.7 %all-to-all-start.2 = ((f32[4,2,4,4,2,128]{5,3,2,0,4,1:T(4,128)}), f32[4,2,4,4,2,128]{5,3,2,0,4,1:T(4,128)S(1)}, u32[]{:S(2)}, u32[]{:S(2)}) async-start(f32[4,2,4,4,2,128]{5,3,2,0,4,1:T(4,128)} %copy.49), calls=%async_computation.2 | async-start | bytes 262144 | tf_op jit(solution)/shard_map/all_to_all | solution.py:40
  41.1 9.9 %all-to-all-start.3 = ((f32[4,2,4,4,2,128]{5,3,1,0,4,2:T(4,128)}), f32[4,2,4,4,2,128]{5,3,1,0,4,2:T(4,128)S(1)}, u32[]{:S(2)}, u32[]{:S(2)}) async-start(f32[4,2,4,4,2,128]{5,3,1,0,4,2:T(4,128)} %copy.50), calls=%async_computation.3 | async-start | bytes 262144 | tf_op jit(solution)/shard_map/all_to_all | solution.py:40
  52.0 14.6 %all-to-all-start.4 = ((f32[64,2,128]{2,1,0:T(2,128)}), f32[64,2,128]{2,1,0:T(2,128)S(1)}, u32[]{:S(2)}, u32[]{:S(2)}) async-start(f32[64,2,128]{2,1,0:T(2,128)} %copy.52), calls=%async_computation.4 | async-start | bytes 131072 | tf_op jit(solution)/shard_map/all_to_all | solution.py:116
  66.9 15.6 %copy-start.1 = (bf16[32,4,8,128]{3,2,1,0:T(8,128)(2,1)S(1)}, bf16[32,4,8,128]{3,2,1,0:T(8,128)(2,1)}, u32[]{:S(2)}) copy-start(bf16[32,4,8,128]{3,2,1,0:T(8,128)(2,1)} %param.5) | copy-start | bytes 786436
  70.5 12.3 %copy-start.3 = (bf16[4,8,128]{2,1,0:T(8,128)(2,1)S(1)}, bf16[4,8,128]{2,1,0:T(8,128)(2,1)}, u32[]{:S(2)}) copy-start(bf16[4,8,128]{2,1,0:T(8,128)(2,1)} %param.6) | copy-start | bytes 24580
  78.6 12.6 %all-to-all-start.5 = ((bf16[32,2,256]{2,1,0:T(2,128)(2,1)}), bf16[32,2,256]{2,1,0:T(2,128)(2,1)S(1)}, u32[]{:S(2)}, u32[]{:S(2)}) async-start(bf16[32,2,256]{2,1,0:T(2,128)(2,1)} %reshape.647), calls=%async_computation.5 | async-start | bytes 65536 | tf_op jit(solution)/shard_map/all_to_all | solution.py:130
  96.9 33.2 %copy-start.4 = (f32[32]{0:T(128)S(1)}, f32[32]{0:T(128)}, u32[]{:S(2)}) copy-start(f32[32]{0:T(128)} %param.9) | copy-start | bytes 388
  98.0 12.7 %all-to-all-start.6 = ((bf16[128,2,128]{2,1,0:T(2,128)(2,1)}), bf16[128,2,128]{2,1,0:T(2,128)(2,1)S(1)}, u32[]{:S(2)}, u32[]{:S(2)}) async-start(bf16[128,2,128]{2,1,0:T(2,128)(2,1)} %copy.56), calls=%async_computation.6 | async-start | bytes 131072 | tf_op jit(solution)/shard_map/all_to_all | solution.py:137
  112.2 16.6 %all-to-all-start.7 = ((bf16[4,32,4,256]{3,2,1,0:T(4,128)(2,1)}), bf16[4,32,4,256]{3,2,1,0:T(4,128)(2,1)S(1)}, u32[]{:S(2)}, u32[]{:S(2)}) async-start(bf16[4,32,4,256]{3,2,1,0:T(4,128)(2,1)} %broadcast_in_dim.2), calls=%async_computation.7 | async-start | bytes 524288 | tf_op jit(solution)/shard_map/all_to_all | solution.py:51
where the time goes:
time: 134 us; the launch traced here: 133 us
  waiting for transfers between devices  40.6 us (30%)
  starting transfers between devices  38.1 us (28%)
  local copies, waits for them, and re-layouts  30.5 us (23%)
  blocking collectives  12 us (9%)
  matrix products  6.59 us (5%)
  other arithmetic  4.99 us (4%)
    all_to_all x3, starting transfers between devices, exchange_in_order(): out = lax.all_to_all(out, axes[k], k, k, tiled=True)  13.1 us
    all_to_all x1, blocking collectives, summed_on_arrival(): parts = lax.all_to_all(in_blocks(x, dim, peers), axis, 0, 0, tiled=True)  12 us
    all_to_all x1, starting transfers between devices, from_everyone(): return lax.all_to_all(copies, axis, split_axis=0, concat_axis=0, tiled=True)  11.5 us
    all_to_all x3, waiting for transfers between devices, exchange_in_order(): out = lax.all_to_all(out, axes[k], k, k, tiled=True)  9.87 us
    all_to_all x1, waiting for transfers between devices, on_device(): lax.all_to_all(cells.astype(jnp.bfloat16), GX, split_axis=0, concat_axis=...  8.82 us
    unnamed x17, local copies, waits for them, and re-layouts  8.78 us
    all_to_all x1, waiting for transfers between devices, on_device(): lax.all_to_all(spectra, GX, split_axis=0, concat_axis=2, tiled=True)  8.57 us
    all_to_all x1, waiting for transfers between devices, on_device(): lax.all_to_all(pencils, GX, split_axis=2, concat_axis=0, tiled=True)  8.38 us
  transfers between devices with their start and end apart: 7, of which 7 were waited for; matrix products, arithmetic and copies ran while one was open for 4% of the time, Pallas kernels for 0%

commit v1 on v0

v1 whole, which is shorter than its diff:
```python
import functools

import jax
import jax.numpy as jnp
import numpy as np
from jax import lax
from jax.experimental import pallas as pl
from jax.experimental.pallas import tpu as pltpu
from jax.sharding import PartitionSpec as P

MESH = pl.DeviceIdType.MESH
BF = jnp.bfloat16
F32 = jnp.float32

NT = (((1,), (1,)), ((), ()))
TN = (((0,), (0,)), ((), ()))
NN = (((1,), (0,)), ((), ()))


def mm(a, b, dims=NN):
    return lax.dot_general(a, b, dims, preferred_element_type=F32)


def freq(n):
    j = np.arange(n)
    return np.where(j < n // 2, j, j - n)


def turn(a, b, n):
    return 2.0 * np.pi / n * ((a * b) % n)


def parts(z):
    return np.stack([z.real, z.imag])


def tables():
    eye4, eye8 = np.eye(4), np.eye(8)
    z, kz = np.arange(128), np.arange(32)
    a = parts(np.exp(-1j * turn(kz[:, None], z[None, :], 128)))
    tz = np.einsum("rkz,xw->rkxwz", a, eye4).reshape(256, 512)
    x = 4 * (4 * np.arange(8)[None, :, None] + np.arange(4)[:, None, None]) + np.arange(4)
    kx = freq(64).reshape(32, 2).T
    th = turn(kx[None, None, None, :, :], x[:, :, :, None, None], 128)
    cs = np.stack([np.cos(th), np.sin(th)])
    tx = np.einsum("sZYxlg,cd->ZslgcYdx", cs, eye4).reshape(4, 512, 128)
    y = np.arange(32).reshape(4, 8)
    ky = freq(16).reshape(4, 4)
    ph = turn(y[:, :, None, None], ky[None, None], 32)
    unit = np.array([1.0, 1j])
    co = np.einsum("hyHk,s,r->hyHksr", np.exp(-1j * ph), np.conj(unit), unit)
    ty = np.einsum("qhyHksr,cd->shrcyHkqd", parts(co), eye8).reshape(1024, 256)
    txi = np.einsum("sZYxlg,cd->ZsYcxlgd", cs, eye4).reshape(4, 256, 256)
    co = np.einsum("HyhK,s,r->HyhKsr", np.exp(1j * ph), unit, unit)
    tyi = np.einsum("qHyhKsr,bd->shbKrHqdy", parts(co), eye8).reshape(512, 512)
    b = np.exp(1j * turn(kz[:, None], z[None, :], 128)) * 2.0**-7.5
    tzi = np.einsum("rkz,xw->rkxwz", np.stack([b.real, -b.imag]), eye4).reshape(256, 512)
    return [jnp.asarray(np.asarray(t, np.float32)).astype(BF) for t in (tz, tx, ty, txi, tyi, tzi)]


def iota(shape, dim):
    return lax.broadcasted_iota(jnp.int32, shape, dim)


def one_hot(cond):
    return jnp.where(cond, 1.0, 0.0).astype(BF)


def cells_by_x(x):
    wide = x.astype(F32).reshape(32, 4, 8, 128)
    return jnp.concatenate([wide[:, k].reshape(256, 128) for k in range(4)], axis=1)


def forward_z(xx, tz):
    out = mm(tz, xx, NT)
    res = []
    for q in range(4):
        lanes = slice(q * 64, q * 64 + 64)
        both = jnp.concatenate([out[:128, lanes], out[128:, lanes]], axis=1)
        res.append(both.astype(BF).reshape(32, 4, 128))
    return res


def before_gelu(wide, xx, diff, point, offset):
    rep = one_hot(iota((256, 32), 0) // 8 == iota((256, 32), 1))
    spread = mm(mm(rep, point).astype(BF), rep, NT)
    same_y = iota((256, 256), 0) % 8 == iota((256, 256), 1) % 8
    kron = jnp.where(same_y, spread, 0.0).astype(BF)
    mix = mm(kron, xx)
    gap = iota((128, 128), 0) - iota((128, 128), 1)
    sten = jnp.where(gap == 0, -2.0, jnp.where((gap == 1) | (gap == -1), 1.0, 0.0)).astype(BF)
    cols = []
    for k in range(4):
        lanes = slice(k * 128, k * 128 + 128)
        curv = mm(xx[:, lanes], sten).reshape(32, 8, 128)
        cols.append((curv * diff[k][None]).reshape(256, 128))
    shift = jnp.concatenate([jnp.full((8, 512), offset(o), F32) for o in range(32)], axis=0)
    return mix + jnp.concatenate(cols, axis=1) + shift


def forward_xy(r1, tx, ty):
    r1 = r1.reshape(512, 128)
    d = jnp.concatenate([r1[h * 128 : h * 128 + 128] for h in range(4)], axis=1)
    g = mm(tx, d).astype(BF)
    g = jnp.concatenate([g[:256], g[256:]], axis=1)
    o = mm(g, ty)
    res = []
    for h in range(4):
        lanes = slice(h * 64, h * 64 + 64)
        both = jnp.concatenate([o[:128, lanes], o[128:, lanes]], axis=1)
        res.append(both.astype(BF).reshape(32, 4, 128))
    return res


def own_modes(r2):
    r2 = r2.reshape(512, 128).astype(F32)
    u = r2[:128] + r2[128:256] + r2[256:384] + r2[384:]
    hi = u.astype(BF)
    lo = (u - hi.astype(F32)).astype(BF)
    row, col = iota((256, 512), 0), iota((256, 512), 1)
    row = row % 128
    rep = one_hot((row % 4 == col // 128) & (row // 4 == col % 32))
    return mm(jnp.concatenate([hi, lo], axis=0), rep, TN) * (2.0**-9.5)


def mix_modes(u, w):
    rows = []
    for j in range(8):
        wr, wi = w(2 * j).astype(F32), w(2 * j + 1).astype(F32)
        re = im = None
        for q in range(4):
            ur = jnp.concatenate([u[16 * j : 16 * j + 8, q * 128 : q * 128 + 128]] * 8, axis=1)
            ui = jnp.concatenate([u[16 * j + 8 : 16 * j + 16, q * 128 : q * 128 + 128]] * 8, axis=1)
            r, i = wr[q * 8 : q * 8 + 8], wi[q * 8 : q * 8 + 8]
            a, b = r * ur - i * ui, r * ui + i * ur
            re, im = (a, b) if re is None else (re + a, im + b)
        rows += [jnp.sum(re, axis=0, keepdims=True), jnp.sum(im, axis=0, keepdims=True)]
    y = jnp.concatenate(rows, axis=0)
    a = jnp.concatenate(
        [y[l * 8 : l * 8 + 8, b * 128 : b * 128 + 128] for l in range(2) for b in range(8)], axis=0
    ).astype(BF)
    row, col = iota((128, 128), 0), iota((128, 128), 1)
    perm = one_hot((row % 4 == col // 32) & (row // 4 == col % 32))
    return mm(perm, a, NT).astype(BF).reshape(32, 4, 128)


def inverse_xy(r3, txi, tyi):
    r3 = r3.reshape(512, 128)
    d = jnp.concatenate(
        [
            jnp.concatenate([r3[h * 128 : h * 128 + 128, l * 64 : l * 64 + 64] for h in range(4)], axis=1)
            for l in range(2)
        ],
        axis=0,
    )
    g = mm(txi, d).astype(BF)
    o = mm(jnp.concatenate([g[:128], g[128:]], axis=1), tyi).astype(BF)
    return [o[:, h * 128 : h * 128 + 128].reshape(8, 4, 4, 128) for h in range(4)]


def inverse_z(r4, tzi):
    halves = [
        jnp.concatenate([r4[o].reshape(128, 128)[:, r * 64 : r * 64 + 64] for o in range(4)], axis=1)
        for r in range(2)
    ]
    res = mm(jnp.concatenate(halves, axis=0), tzi, TN)
    return jnp.transpose(res.reshape(4, 8, 8, 512), (1, 0, 2, 3)).reshape(256, 512)


def gelu(v):
    return 0.5 * v * (1.0 + lax.erf(v * (0.5**0.5)))


def far_first(sizes):
    steps = [()]
    for n in sizes:
        steps = [s + (k,) for s in steps for k in range(n)]
    steps = [s + (c,) for s in steps for c in range(2)]
    steps.sort(key=lambda s: (-sum(min(k, n - k) for k, n in zip(s, sizes)), -s[-1]))
    return steps[:-1]


def kernel(
    x_hbm, diff_hbm, w_hbm, point_ref, off_ref, tz_hbm, tx_hbm, ty_hbm, txi_hbm, tyi_hbm, tzi_hbm,
    out_ref,
    x_v, diff_v, w_v, tz_v, tx_v, ty_v, txi_v, tyi_v, tzi_v, pre_v,
    s1, r1, s2, r2, s3, r3, s4, r4, load_sem, send_sem, recv_sem,
):
    g, h = lax.axis_index("gx"), lax.axis_index("gy")
    plane, zz = g // 4, g % 4
    kz = plane * 4 + h
    yy, xc, core = g // 8, (plane % 2) * 2 + h // 2, h % 2
    ys = [lax.rem(yy + k, 4) * 8 for k in range(4)]
    zs = [lax.rem(zz + k, 4) for k in range(4)]
    xs = [lax.rem(xc + k, 4) for k in range(4)]
    ups = [[ys[a] + xs[b] // 2 * 4 for b in range(4)] for a in range(4)]
    gys = [[xs[b] % 2 * 2 + c for c in (core, 1 - core)] for b in range(4)]
    everyone = [(ups[a][b] + zs[c], gys[b][d]) for a, b, c, d in far_first((4, 4, 4))]
    planar = [(ups[a][b], gys[b][d]) for a, b, d in far_first((4, 4))]

    barrier = pltpu.get_barrier_semaphore()
    for peer in everyone:
        pl.semaphore_signal(barrier, inc=1, device_id=peer, device_id_type=MESH)

    loads = [
        (x_hbm, x_v), (tz_hbm, tz_v), (diff_hbm, diff_v), (tx_hbm.at[zz], tx_v), (ty_hbm, ty_v),
        (w_hbm, w_v), (txi_hbm.at[zz], txi_v), (tyi_hbm, tyi_v), (tzi_hbm, tzi_v),
    ]
    loads = [pltpu.make_async_copy(a, b, load_sem.at[k]) for k, (a, b) in enumerate(loads)]
    for c in loads:
        c.start()
    loads[0].wait()
    loads[1].wait()
    xx = cells_by_x(x_v[...]).astype(BF)
    for q, block in enumerate(forward_z(xx, tz_v[...])):
        s1[:, q] = block
    loads[2].wait()
    diff = diff_v[...].astype(F32)
    pre_v[...] = before_gelu(None, xx, diff, point_ref[...], lambda o: off_ref[o])
    for c in loads[3:]:
        c.wait()
    pl.semaphore_wait(barrier, 127)

    def send(src, dst, phase, peer):
        pltpu.make_async_remote_copy(
            src, dst, send_sem.at[phase], recv_sem.at[phase], device_id=peer, device_id_type=MESH
        ).start()

    def wait(ref, sem):
        pltpu.make_async_copy(ref, ref, sem).wait()

    slot = h * 8 + plane
    for up, gy in planar:
        send(s1.at[up + gy], r1.at[slot], 0, (up + zz, gy))
    r1[slot] = s1[kz]
    wait(r1.at[pl.ds(0, 31)], recv_sem.at[0])

    for k, block in enumerate(forward_xy(r1[...], tx_v[...], ty_v[...])):
        s2[k] = block
    slot = zz * 32 + kz
    for gx, gy in everyone:
        send(s2.at[gy, gx], r2.at[slot], 1, (gx, gy))
    r2[slot] = s2[h, g]
    wait(r2.at[pl.ds(0, 127)], recv_sem.at[1])

    s3[...] = mix_modes(own_modes(r2[...]), lambda m: w_v[m])
    slot = h * 32 + g
    for a, b, c, d in far_first((4, 4, 4)):
        up, gy = ups[a][b], gys[b][d]
        send(s3.at[up + gy], r3.at[slot], 2, (up + zs[c], gy))
    r3[slot] = s3[kz]
    wait(r3.at[pl.ds(0, 127)], recv_sem.at[2])

    for k, block in enumerate(inverse_xy(r3[...], txi_v[...], tyi_v[...])):
        s4[:, k] = block
    for up, gy in planar:
        send(s4.at[up // 4, gy], r4.at[:, kz], 3, (up + zz, gy))
    r4[:, kz] = s4[plane, h]
    wait(r1.at[pl.ds(0, 31)], recv_sem.at[3])

    act = gelu(pre_v[...] + inverse_z(r4[...], tzi_v[...]))
    act = jnp.stack([act[:, k * 128 : k * 128 + 128].reshape(32, 8, 128) for k in range(4)], axis=1)
    out_ref[...] = act.reshape(1024, 128).astype(BF)

    wait(s1.at[pl.ds(0, 31)], send_sem.at[0])
    wait(r2.at[pl.ds(0, 127)], send_sem.at[1])
    wait(r2.at[pl.ds(0, 127)], send_sem.at[2])
    wait(s1.at[pl.ds(0, 31)], send_sem.at[3])


def on_device(inputs, diffusion, spectral, pointwise, offsets):
    hbm = pl.BlockSpec(memory_space=pl.ANY)
    vmem = pl.BlockSpec(memory_space=pltpu.VMEM)
    smem = pl.BlockSpec(memory_space=pltpu.SMEM)
    v = pltpu.VMEM
    out = pl.pallas_call(
        kernel,
        out_shape=jax.ShapeDtypeStruct((1024, 128), BF),
        in_specs=[hbm, hbm, hbm, vmem, smem] + [hbm] * 6,
        out_specs=vmem,
        scratch_shapes=[
            v((1024, 128), BF), v((4, 8, 128), BF), v((16, 32, 1024), BF),
            v((256, 512), BF), v((512, 128), BF), v((1024, 256), BF),
            v((256, 256), BF), v((512, 512), BF), v((256, 512), BF), v((256, 512), F32),
            v((32, 4, 4, 128), BF), v((32, 4, 4, 128), BF),
            v((4, 32, 4, 128), BF), v((128, 4, 128), BF),
            v((32, 4, 128), BF), v((128, 4, 128), BF),
            v((8, 4, 4, 4, 128), BF), v((4, 32, 4, 128), BF),
            pltpu.SemaphoreType.DMA((9,)), pltpu.SemaphoreType.DMA((4,)), pltpu.SemaphoreType.DMA((4,)),
        ],
        compiler_params=pltpu.CompilerParams(
            collective_id=0, has_side_effects=True, vmem_limit_bytes=50 << 20
        ),
    )(
        inputs.reshape(1024, 128),
        diffusion,
        spectral.reshape(16, 32, 1024),
        pointwise,
        offsets,
        *tables(),
    )
    return out.reshape(32, 4, 8, 128)


def solution(mesh):
    return jax.shard_map(
        on_device,
        mesh=mesh,
        in_specs=(P(None, "gx", "gy", None), P("gx", "gy", None), P("gx", "gy", None, None, None), P(), P()),
        out_specs=P(None, "gx", "gy", None),
        check_vma=False,
    )
```

time: 134 us -> 45.1 us (0.34)
  waiting for transfers between devices: 40.6 us -> 0 us
  starting transfers between devices: 38.1 us -> 0 us
  Pallas kernels: 0 us -> 34.8 us
  local copies, waits for them, and re-layouts: 30.5 us -> 9.77 us
  blocking collectives: 12 us -> 0 us
  matrix products: 6.59 us -> 0 us
  other arithmetic: 4.99 us -> 0 us
    all_to_all x7 -> x0, waiting for transfers between devices: 40.6 us -> none  [the longest x3 9.87 us: exchange_in_order(): out = lax.all_to_all(out, axes[k], k, k, tiled=True)]
    all_to_all x7 -> x0, starting transfers between devices: 38.1 us -> none  [the longest x3 13.1 us: exchange_in_order(): out = lax.all_to_all(out, axes[k], k, k, tiled=True)]
    pallas_call x0 -> x1, Pallas kernels: none -> 34.8 us  [on_device(): pl.pallas_call(kernel, out_shape=jax.ShapeDtypeStruct((1024, 128), BF), i...]
    all_to_all x1 -> x0, blocking collectives: 12 us -> none  [summed_on_arrival(): parts = lax.all_to_all(in_blocks(x, dim, peers), axis, 0, 0, tiled=True)]
    reshape x7 -> x0, local copies, waits for them, and re-layouts: 11.5 us -> none  [the longest x1 4.36 us: on_device(): spectral.astype(jnp.float32).reshape(owned_x, owned_y, 2, C, C, MZ)]
    dot_general x7 -> x0, matrix products: 6.59 us -> none  [the longest x1 3.12 us: on_device(): jnp.dot(spatial.reshape(-1, 2 * MZ), z_inverse, precision=highest, prefer...]
    unnamed x1 -> x0, other arithmetic: 3.59 us -> none
    all_to_all x5 -> x0, local copies, waits for them, and re-layouts: 2.62 us -> none  [the longest x3 1.37 us: exchange_in_order(): out = lax.all_to_all(out, axes[k], k, k, tiled=True)]
  transfers between devices with their start and end apart: 7 -> 0, of which waited for: 7 -> 0; matrix products, arithmetic and copies ran while one was open for 4% -> 0% of each run, Pallas kernels for 0% -> 0%
where the time goes in v1:
time: 45.1 us; the launch traced here: 44.5 us
  Pallas kernels  34.8 us (77%)
  local copies, waits for them, and re-layouts  9.77 us (22%)
    pallas_call x1, Pallas kernels, on_device(): pl.pallas_call(kernel, out_shape=jax.ShapeDtypeStruct((1024, 128), BF), i...  34.8 us
    unnamed x21, local copies, waits for them, and re-layouts  9.77 us

profile of v1, /device:TPU:1, one launch (start us, length us, event | category | flops | bytes accessed | tf_op | source)
XLA Modules:
  0.0 44.5 jit_solution(10400289008035242131)
XLA Ops:
  0.0 0.0 copy-start.9
  0.0 0.7 %copy-done.9 = f32[32]{0:T(128)S(1)} copy-done((f32[32]{0:T(128)S(1)}, f32[32]{0:T(128)}, u32[]{:S(2)}) %copy-start.9) | copy-done | bytes 152
  0.7 0.0 copy-start
  0.7 1.0 %copy-done = bf16[512,512]{1,0:T(8,128)(2,1)S(1)} copy-done((bf16[512,512]{1,0:T(8,128)(2,1)S(1)}, bf16[512,512]{1,0:T(8,128)(2,1)}, u32[]{:S(2)}) %copy-start) | copy-done | bytes 524312
  1.7 0.0 copy-start.1
  1.7 1.0 %copy-done.1 = bf16[4,256,256]{2,1,0:T(8,128)(2,1)S(1)} copy-done((bf16[4,256,256]{2,1,0:T(8,128)(2,1)S(1)}, bf16[4,256,256]{2,1,0:T(8,128)(2,1)}, u32[]{:S(2)}) %copy-start.1) | copy-done | bytes 524312
  2.7 0.0 copy-start.2
  2.7 1.0 %copy-done.2 = bf16[1024,256]{1,0:T(8,128)(2,1)S(1)} copy-done((bf16[1024,256]{1,0:T(8,128)(2,1)S(1)}, bf16[1024,256]{1,0:T(8,128)(2,1)}, u32[]{:S(2)}) %copy-start.2) | copy-done | bytes 524312
  3.8 0.0 copy-start.3
  3.8 1.0 %copy-done.3 = bf16[4,512,128]{2,1,0:T(8,128)(2,1)S(1)} copy-done((bf16[4,512,128]{2,1,0:T(8,128)(2,1)S(1)}, bf16[4,512,128]{2,1,0:T(8,128)(2,1)}, u32[]{:S(2)}) %copy-start.3) | copy-done | bytes 524312
  4.8 0.0 copy-start.4
  4.8 0.9 %copy-done.4 = bf16[32,4,8,128]{3,2,1,0:T(8,128)(2,1)S(1)} copy-done((bf16[32,4,8,128]{3,2,1,0:T(8,128)(2,1)S(1)}, bf16[32,4,8,128]{3,2,1,0:T(8,128)(2,1)}, u32[]{:S(2)}) %copy-start.4) | copy-done | bytes 262168
  5.8 0.0 copy-start.5
  5.8 0.9 %copy-done.5 = bf16[256,512]{1,0:T(8,128)(2,1)S(1)} copy-done((bf16[256,512]{1,0:T(8,128)(2,1)S(1)}, bf16[256,512]{1,0:T(8,128)(2,1)}, u32[]{:S(2)}) %copy-start.5) | copy-done | bytes 262168
  6.7 0.0 copy-start.6
  6.7 0.9 %copy-done.6 = bf16[256,512]{1,0:T(8,128)(2,1)S(1)} copy-done((bf16[256,512]{1,0:T(8,128)(2,1)S(1)}, bf16[256,512]{1,0:T(8,128)(2,1)}, u32[]{:S(2)}) %copy-start.6) | copy-done | bytes 262168
  7.7 0.0 copy-start.7
  7.7 0.7 %copy-done.7 = bf16[4,8,128]{2,1,0:T(8,128)(2,1)S(1)} copy-done((bf16[4,8,128]{2,1,0:T(8,128)(2,1)S(1)}, bf16[4,8,128]{2,1,0:T(8,128)(2,1)}, u32[]{:S(2)}) %copy-start.7) | copy-done | bytes 8216
  8.4 0.0 copy-start.8
  8.4 0.7 %copy-done.8 = bf16[32,32]{1,0:T(8,128)(2,1)S(1)} copy-done((bf16[32,32]{1,0:T(8,128)(2,1)S(1)}, bf16[32,32]{1,0:T(8,128)(2,1)}, u32[]{:S(2)}) %copy-start.8) | copy-done | bytes 2072
  9.1 34.8 %shard_map.109 = bf16[1024,128]{1,0:T(8,128)(2,1)S(1)} custom-call(bf16[1024,128]{1,0:T(8,128)(2,1)S(1)} %bitcast.4, bf16[4,8,128]{2,1,0:T(8,128)(2,1)S(1)} %copy-done.7, bf16[16,32,1024]{2,1,0:T(8,128)(2,1)} %bitcast.5, bf16[32,32]{1,0:T(8,128)(2,1)S(1)} %copy-done.8, f32[32]{0:T(128)S(1)} %copy-done.9, bf16[256,512]{1,0:T(8,128)(2,1)S(1)} %copy-done.6, ...), custom_call_target="tpu_custom_call" | custom-call | tf_op jit(solution)/shard_map/pallas_call | solution.py:276
  43.8 0.7 %copy.13 = bf16[32,4,8,128]{3,2,1,0:T(8,128)(2,1)} copy(bf16[32,4,8,128]{3,2,1,0:T(8,128)(2,1)S(1)} %bitcast.3) | data formatting | bytes 524288
Async XLA Ops:
  0.0 0.7 %copy-start.9 = (f32[32]{0:T(128)S(1)}, f32[32]{0:T(128)}, u32[]{:S(2)}) copy-start(f32[32]{0:T(128)} %off_ref.1) | copy-start | bytes 388
  0.7 1.0 %copy-start = (bf16[512,512]{1,0:T(8,128)(2,1)S(1)}, bf16[512,512]{1,0:T(8,128)(2,1)}, u32[]{:S(2)}) copy-start(bf16[512,512]{1,0:T(8,128)(2,1)} %constant.25.tyi_hbm) | copy-start | bytes 1572868
  1.7 1.0 %copy-start.1 = (bf16[4,256,256]{2,1,0:T(8,128)(2,1)S(1)}, bf16[4,256,256]{2,1,0:T(8,128)(2,1)}, u32[]{:S(2)}) copy-start(bf16[4,256,256]{2,1,0:T(8,128)(2,1)} %constant.24.txi_hbm) | copy-start | bytes 1572868
  2.7 1.0 %copy-start.2 = (bf16[1024,256]{1,0:T(8,128)(2,1)S(1)}, bf16[1024,256]{1,0:T(8,128)(2,1)}, u32[]{:S(2)}) copy-start(bf16[1024,256]{1,0:T(8,128)(2,1)} %constant.23.ty_hbm) | copy-start | bytes 1572868
  3.8 1.0 %copy-start.3 = (bf16[4,512,128]{2,1,0:T(8,128)(2,1)S(1)}, bf16[4,512,128]{2,1,0:T(8,128)(2,1)}, u32[]{:S(2)}) copy-start(bf16[4,512,128]{2,1,0:T(8,128)(2,1)} %constant.22.tx_hbm) | copy-start | bytes 1572868
  4.8 0.9 %copy-start.4 = (bf16[32,4,8,128]{3,2,1,0:T(8,128)(2,1)S(1)}, bf16[32,4,8,128]{3,2,1,0:T(8,128)(2,1)}, u32[]{:S(2)}) copy-start(bf16[32,4,8,128]{3,2,1,0:T(8,128)(2,1)} %param.11) | copy-start | bytes 786436
  5.8 0.9 %copy-start.5 = (bf16[256,512]{1,0:T(8,128)(2,1)S(1)}, bf16[256,512]{1,0:T(8,128)(2,1)}, u32[]{:S(2)}) copy-start(bf16[256,512]{1,0:T(8,128)(2,1)} %constant.26.tzi_hbm) | copy-start | bytes 786436
  6.7 0.9 %copy-start.6 = (bf16[256,512]{1,0:T(8,128)(2,1)S(1)}, bf16[256,512]{1,0:T(8,128)(2,1)}, u32[]{:S(2)}) copy-start(bf16[256,512]{1,0:T(8,128)(2,1)} %constant.21.tz_hbm) | copy-start | bytes 786436
  7.7 0.7 %copy-start.7 = (bf16[4,8,128]{2,1,0:T(8,128)(2,1)S(1)}, bf16[4,8,128]{2,1,0:T(8,128)(2,1)}, u32[]{:S(2)}) copy-start(bf16[4,8,128]{2,1,0:T(8,128)(2,1)} %diff_hbm.1) | copy-start | bytes 24580
  8.4 0.7 %copy-start.8 = (bf16[32,32]{1,0:T(8,128)(2,1)S(1)}, bf16[32,32]{1,0:T(8,128)(2,1)}, u32[]{:S(2)}) copy-start(bf16[32,32]{1,0:T(8,128)(2,1)} %point_ref.1) | copy-start | bytes 6148

commit v2 on v1

--- a/solution.py
+++ b/solution.py
@@ -181,9 +181,9 @@
 
 
 def kernel(
-    x_hbm, diff_hbm, w_hbm, point_ref, off_ref, tz_hbm, tx_hbm, ty_hbm, txi_hbm, tyi_hbm, tzi_hbm,
+    x_hbm, diff_hbm, w_hbm, point_hbm, off_hbm, tz_hbm, tx_hbm, ty_hbm, txi_hbm, tyi_hbm, tzi_hbm,
     out_ref,
-    x_v, diff_v, w_v, tz_v, tx_v, ty_v, txi_v, tyi_v, tzi_v, pre_v,
+    x_v, diff_v, w_v, point_ref, off_ref, tz_v, tx_v, ty_v, txi_v, tyi_v, tzi_v, pre_v,
     s1, r1, s2, r2, s3, r3, s4, r4, load_sem, send_sem, recv_sem,
 ):
     g, h = lax.axis_index("gx"), lax.axis_index("gy")
@@ -203,7 +203,7 @@
         pl.semaphore_signal(barrier, inc=1, device_id=peer, device_id_type=MESH)
 
     loads = [
-        (x_hbm, x_v), (tz_hbm, tz_v), (diff_hbm, diff_v), (tx_hbm.at[zz], tx_v), (ty_hbm, ty_v),
+        (x_hbm, x_v), (tz_hbm, tz_v), (diff_hbm, diff_v), (point_hbm, point_ref), (off_hbm, off_ref), (tx_hbm.at[zz], tx_v), (ty_hbm, ty_v),
         (w_hbm, w_v), (txi_hbm.at[zz], txi_v), (tyi_hbm, tyi_v), (tzi_hbm, tzi_v),
     ]
     loads = [pltpu.make_async_copy(a, b, load_sem.at[k]) for k, (a, b) in enumerate(loads)]
@@ -214,10 +214,11 @@
     xx = cells_by_x(x_v[...]).astype(BF)
     for q, block in enumerate(forward_z(xx, tz_v[...])):
         s1[:, q] = block
-    loads[2].wait()
+    for c in loads[2:5]:
+        c.wait()
     diff = diff_v[...].astype(F32)
     pre_v[...] = before_gelu(None, xx, diff, point_ref[...], lambda o: off_ref[o])
-    for c in loads[3:]:
+    for c in loads[5:]:
         c.wait()
     pl.semaphore_wait(barrier, 127)
 
@@ -269,27 +270,26 @@
 
 
 def on_device(inputs, diffusion, spectral, pointwise, offsets):
-    hbm = pl.BlockSpec(memory_space=pl.ANY)
+    hbm = pl.BlockSpec(memory_space=pltpu.HBM)
     vmem = pl.BlockSpec(memory_space=pltpu.VMEM)
-    smem = pl.BlockSpec(memory_space=pltpu.SMEM)
     v = pltpu.VMEM
     out = pl.pallas_call(
         kernel,
         out_shape=jax.ShapeDtypeStruct((1024, 128), BF),
-        in_specs=[hbm, hbm, hbm, vmem, smem] + [hbm] * 6,
+        in_specs=[hbm] * 11,
         out_specs=vmem,
         scratch_shapes=[
-            v((1024, 128), BF), v((4, 8, 128), BF), v((16, 32, 1024), BF),
+            v((1024, 128), BF), v((4, 8, 128), BF), v((16, 32, 1024), BF), v((32, 32), BF), pltpu.SMEM((32,), F32),
             v((256, 512), BF), v((512, 128), BF), v((1024, 256), BF),
             v((256, 256), BF), v((512, 512), BF), v((256, 512), BF), v((256, 512), F32),
             v((32, 4, 4, 128), BF), v((32, 4, 4, 128), BF),
             v((4, 32, 4, 128), BF), v((128, 4, 128), BF),
             v((32, 4, 128), BF), v((128, 4, 128), BF),
             v((8, 4, 4, 4, 128), BF), v((4, 32, 4, 128), BF),
-            pltpu.SemaphoreType.DMA((9,)), pltpu.SemaphoreType.DMA((4,)), pltpu.SemaphoreType.DMA((4,)),
+            pltpu.SemaphoreType.DMA((11,)), pltpu.SemaphoreType.DMA((4,)), pltpu.SemaphoreType.DMA((4,)),
         ],
         compiler_params=pltpu.CompilerParams(
-            collective_id=0, has_side_effects=True, vmem_limit_bytes=50 << 20
+            collective_id=0, has_side_effects=True, vmem_limit_bytes=60 << 20
         ),
     )(
         inputs.reshape(1024, 128),

time: 45.1 us -> 36.6 us (0.81)
  local copies, waits for them, and re-layouts: 9.77 us -> 1.67 us
    unnamed x21 -> x1, local copies, waits for them, and re-layouts: 9.77 us -> 1.67 us
where the time goes in v2:
time: 36.6 us; the launch traced here: 36.4 us
  Pallas kernels  34.7 us (95%)
  local copies, waits for them, and re-layouts  1.67 us (5%)
    pallas_call x1, Pallas kernels, on_device(): pl.pallas_call(kernel, out_shape=jax.ShapeDtypeStruct((1024, 128), BF), i...  34.7 us
    unnamed x1, local copies, waits for them, and re-layouts  1.67 us

profile of v2, /device:TPU:1, one launch (start us, length us, event | category | flops | bytes accessed | tf_op | source)
XLA Modules:
  0.0 36.4 jit_solution(18152050012781122390)
XLA Ops:
  0.0 34.7 %shard_map.109 = bf16[1024,128]{1,0:T(8,128)(2,1)} custom-call(bf16[1024,128]{1,0:T(8,128)(2,1)} %bitcast.5, bf16[4,8,128]{2,1,0:T(8,128)(2,1)} %diff_hbm.1, bf16[16,32,1024]{2,1,0:T(8,128)(2,1)} %bitcast.3, bf16[32,32]{1,0:T(8,128)(2,1)} %point_hbm.1, f32[32]{0:T(128)} %off_hbm.1, bf16[256,512]{1,0:T(8,128)(2,1)} %constant.21.tz_hbm, ...), custom_call_target="tpu_custom_call" | custom-call | tf_op jit(solution)/shard_map/pallas_call | solution.py:276
  34.7 1.7 %copy.13 = bf16[32,4,8,128]{3,2,1,0:T(8,128)(2,1)} copy(bf16[32,4,8,128]{3,2,1,0:T(8,128)(2,1)} %bitcast.4) | data formatting | bytes 524288

commit v3 on v2

--- a/solution.py
+++ b/solution.py
@@ -273,6 +273,7 @@
     hbm = pl.BlockSpec(memory_space=pltpu.HBM)
     vmem = pl.BlockSpec(memory_space=pltpu.VMEM)
     v = pltpu.VMEM
+    args = [inputs.reshape(1024, 128), diffusion, spectral.reshape(16, 32, 1024), pointwise, offsets, *tables()]
     out = pl.pallas_call(
         kernel,
         out_shape=jax.ShapeDtypeStruct((1024, 128), BF),
@@ -289,16 +290,9 @@
             pltpu.SemaphoreType.DMA((11,)), pltpu.SemaphoreType.DMA((4,)), pltpu.SemaphoreType.DMA((4,)),
         ],
         compiler_params=pltpu.CompilerParams(
-            collective_id=0, has_side_effects=True, vmem_limit_bytes=60 << 20
+            collective_id=0, has_side_effects=True, vmem_limit_bytes=40 << 20
         ),
-    )(
-        inputs.reshape(1024, 128),
-        diffusion,
-        spectral.reshape(16, 32, 1024),
-        pointwise,
-        offsets,
-        *tables(),
-    )
+    )(*[pltpu.with_memory_space_constraint(a, pltpu.HBM) for a in args])
     return out.reshape(32, 4, 8, 128)
 
 

time: 36.6 us -> 34.9 us (0.954)
  local copies, waits for them, and re-layouts: 1.67 us -> 0.71 us
  Pallas kernels: 34.7 us -> 34.1 us
    unnamed x1, local copies, waits for them, and re-layouts: 1.67 us -> 0.71 us
    pallas_call x1, Pallas kernels: 34.7 us -> 34.1 us  [on_device(): pl.pallas_call(kernel, out_shape=jax.ShapeDtypeStruct((1024, 128), BF), i...]
where the time goes in v3:
time: 34.9 us; the launch traced here: 34.8 us
  Pallas kernels  34.1 us (98%)
  local copies, waits for them, and re-layouts  0.71 us (2%)
    pallas_call x1, Pallas kernels, on_device(): pl.pallas_call(kernel, out_shape=jax.ShapeDtypeStruct((1024, 128), BF), i...  34.1 us
    unnamed x1, local copies, waits for them, and re-layouts  0.71 us

profile of v3, /device:TPU:1, one launch (start us, length us, event | category | flops | bytes accessed | tf_op | source)
XLA Modules:
  0.0 34.8 jit_solution(5734080794223687932)
XLA Ops:
  0.0 34.1 %shard_map.109 = bf16[1024,128]{1,0:T(8,128)(2,1)S(1)} custom-call(bf16[1024,128]{1,0:T(8,128)(2,1)} %bitcast.5, bf16[4,8,128]{2,1,0:T(8,128)(2,1)} %diff_hbm.1, bf16[16,32,1024]{2,1,0:T(8,128)(2,1)} %bitcast.4, bf16[32,32]{1,0:T(8,128)(2,1)} %point_hbm.1, f32[32]{0:T(128)} %off_hbm.1, bf16[256,512]{1,0:T(8,128)(2,1)} %constant.21.tz_hbm, ...), custom_call_target="tpu_custom_call" | custom-call | tf_op jit(solution)/shard_map/pallas_call | solution.py:277
  34.1 0.7 %copy.13 = bf16[32,4,8,128]{3,2,1,0:T(8,128)(2,1)} copy(bf16[32,4,8,128]{3,2,1,0:T(8,128)(2,1)S(1)} %bitcast.3) | data formatting | bytes 524288

commit v4 on v3

--- a/solution.py
+++ b/solution.py
@@ -39,17 +39,17 @@
     z, kz = np.arange(128), np.arange(32)
     a = parts(np.exp(-1j * turn(kz[:, None], z[None, :], 128)))
     tz = np.einsum("rkz,xw->rkxwz", a, eye4).reshape(256, 512)
+    unit = np.array([1.0, 1j])
+    y = np.arange(32).reshape(4, 8)
+    ky = freq(16).reshape(4, 4)
+    ph = turn(y[:, :, None, None], ky[None, None], 32)
+    co = np.einsum("hyHk,s,r->hyHksr", np.exp(-1j * ph), np.conj(unit), unit)
+    ty = np.einsum("qhyHksr,cd->hrcysHkqd", parts(co), eye8).reshape(512, 512)
     x = 4 * (4 * np.arange(8)[None, :, None] + np.arange(4)[:, None, None]) + np.arange(4)
     kx = freq(64).reshape(32, 2).T
     th = turn(kx[None, None, None, :, :], x[:, :, :, None, None], 128)
     cs = np.stack([np.cos(th), np.sin(th)])
-    tx = np.einsum("sZYxlg,cd->ZslgcYdx", cs, eye4).reshape(4, 512, 128)
-    y = np.arange(32).reshape(4, 8)
-    ky = freq(16).reshape(4, 4)
-    ph = turn(y[:, :, None, None], ky[None, None], 32)
-    unit = np.array([1.0, 1j])
-    co = np.einsum("hyHk,s,r->hyHksr", np.exp(-1j * ph), np.conj(unit), unit)
-    ty = np.einsum("qhyHksr,cd->shrcyHkqd", parts(co), eye8).reshape(1024, 256)
+    tx = np.einsum("sZYxlg,cd->ZlgcsYdx", cs, eye4).reshape(4, 256, 256)
     txi = np.einsum("sZYxlg,cd->ZsYcxlgd", cs, eye4).reshape(4, 256, 256)
     co = np.einsum("HyhK,s,r->HyhKsr", np.exp(1j * ph), unit, unit)
     tyi = np.einsum("qHyhKsr,bd->shbKrHqdy", parts(co), eye8).reshape(512, 512)
@@ -101,9 +101,8 @@
 def forward_xy(r1, tx, ty):
     r1 = r1.reshape(512, 128)
     d = jnp.concatenate([r1[h * 128 : h * 128 + 128] for h in range(4)], axis=1)
-    g = mm(tx, d).astype(BF)
-    g = jnp.concatenate([g[:256], g[256:]], axis=1)
-    o = mm(g, ty)
+    e = mm(d, ty).astype(BF)
+    o = mm(tx, jnp.concatenate([e[:, :256], e[:, 256:]], axis=0))
     res = []
     for h in range(4):
         lanes = slice(h * 64, h * 64 + 64)
@@ -123,22 +122,37 @@
     return mm(jnp.concatenate([hi, lo], axis=0), rep, TN) * (2.0**-9.5)
 
 
+def sum_rows(acc):
+    row = iota(acc[0].shape, 0)
+    half = row < 4
+    four = [
+        jnp.where(half, acc[k], acc[k + 4]) + pltpu.roll(jnp.where(half, acc[k + 4], acc[k]), 4, 0)
+        for k in range(4)
+    ]
+
+    def join(a, b, k):
+        return jnp.where(row % (2 * k) < k, a + pltpu.roll(a, 8 - k, 0), b + pltpu.roll(b, k, 0))
+
+    return join(join(four[0], four[2], 2), join(four[1], four[3], 2), 1)
+
+
 def mix_modes(u, w):
-    rows = []
-    for j in range(8):
-        wr, wi = w(2 * j).astype(F32), w(2 * j + 1).astype(F32)
-        re = im = None
-        for q in range(4):
-            ur = jnp.concatenate([u[16 * j : 16 * j + 8, q * 128 : q * 128 + 128]] * 8, axis=1)
-            ui = jnp.concatenate([u[16 * j + 8 : 16 * j + 16, q * 128 : q * 128 + 128]] * 8, axis=1)
-            r, i = wr[q * 8 : q * 8 + 8], wi[q * 8 : q * 8 + 8]
-            a, b = r * ur - i * ui, r * ui + i * ur
-            re, im = (a, b) if re is None else (re + a, im + b)
-        rows += [jnp.sum(re, axis=0, keepdims=True), jnp.sum(im, axis=0, keepdims=True)]
-    y = jnp.concatenate(rows, axis=0)
-    a = jnp.concatenate(
-        [y[l * 8 : l * 8 + 8, b * 128 : b * 128 + 128] for l in range(2) for b in range(8)], axis=0
-    ).astype(BF)
+    blocks = []
+    for l in range(2):
+        acc = []
+        for j in range(4 * l, 4 * l + 4):
+            wr, wi = w(2 * j), w(2 * j + 1)
+            re = im = None
+            for q in range(4):
+                ur = jnp.concatenate([u[16 * j : 16 * j + 8, q * 128 : q * 128 + 128]] * 8, axis=1)
+                ui = jnp.concatenate([u[16 * j + 8 : 16 * j + 16, q * 128 : q * 128 + 128]] * 8, axis=1)
+                r, i = wr[q * 8 : q * 8 + 8], wi[q * 8 : q * 8 + 8]
+                a, b = r * ur - i * ui, r * ui + i * ur
+                re, im = (a, b) if re is None else (re + a, im + b)
+            acc += [re, im]
+        y = sum_rows(acc)
+        blocks += [y[:, b * 128 : b * 128 + 128] for b in range(8)]
+    a = jnp.concatenate(blocks, axis=0).astype(BF)
     row, col = iota((128, 128), 0), iota((128, 128), 1)
     perm = one_hot((row % 4 == col // 32) & (row // 4 == col % 32))
     return mm(perm, a, NT).astype(BF).reshape(32, 4, 128)
@@ -183,7 +197,7 @@
 def kernel(
     x_hbm, diff_hbm, w_hbm, point_hbm, off_hbm, tz_hbm, tx_hbm, ty_hbm, txi_hbm, tyi_hbm, tzi_hbm,
     out_ref,
-    x_v, diff_v, w_v, point_ref, off_ref, tz_v, tx_v, ty_v, txi_v, tyi_v, tzi_v, pre_v,
+    x_v, diff_v, w_v, wide_v, point_ref, off_ref, tz_v, tx_v, ty_v, txi_v, tyi_v, tzi_v, pre_v,
     s1, r1, s2, r2, s3, r3, s4, r4, load_sem, send_sem, recv_sem,
 ):
     g, h = lax.axis_index("gx"), lax.axis_index("gy")
@@ -234,6 +248,8 @@
     for up, gy in planar:
         send(s1.at[up + gy], r1.at[slot], 0, (up + zz, gy))
     r1[slot] = s1[kz]
+    for m in range(16):
+        wide_v[m] = w_v[m].astype(F32)
     wait(r1.at[pl.ds(0, 31)], recv_sem.at[0])
 
     for k, block in enumerate(forward_xy(r1[...], tx_v[...], ty_v[...])):
@@ -244,7 +260,7 @@
     r2[slot] = s2[h, g]
     wait(r2.at[pl.ds(0, 127)], recv_sem.at[1])
 
-    s3[...] = mix_modes(own_modes(r2[...]), lambda m: w_v[m])
+    s3[...] = mix_modes(own_modes(r2[...]), lambda m: wide_v[m])
     slot = h * 32 + g
     for a, b, c, d in far_first((4, 4, 4)):
         up, gy = ups[a][b], gys[b][d]
@@ -280,8 +296,8 @@
         in_specs=[hbm] * 11,
         out_specs=vmem,
         scratch_shapes=[
-            v((1024, 128), BF), v((4, 8, 128), BF), v((16, 32, 1024), BF), v((32, 32), BF), pltpu.SMEM((32,), F32),
-            v((256, 512), BF), v((512, 128), BF), v((1024, 256), BF),
+            v((1024, 128), BF), v((4, 8, 128), BF), v((16, 32, 1024), BF), v((16, 32, 1024), F32), v((32, 32), BF), pltpu.SMEM((32,), F32),
+            v((256, 512), BF), v((256, 256), BF), v((512, 512), BF),
             v((256, 256), BF), v((512, 512), BF), v((256, 512), BF), v((256, 512), F32),
             v((32, 4, 4, 128), BF), v((32, 4, 4, 128), BF),
             v((4, 32, 4, 128), BF), v((128, 4, 128), BF),

time: 34.9 us -> 34.6 us (level)
  no operation moved by 1% of the time
where the time goes in v4:
time: 34.6 us; the launch traced here: 34.5 us
  Pallas kernels  33.8 us (98%)
  local copies, waits for them, and re-layouts  0.71 us (2%)
    pallas_call x1, Pallas kernels, on_device(): pl.pallas_call(kernel, out_shape=jax.ShapeDtypeStruct((1024, 128), BF), i...  33.8 us
    unnamed x1, local copies, waits for them, and re-layouts  0.71 us

profile of v4, /device:TPU:1, one launch (start us, length us, event | category | flops | bytes accessed | tf_op | source)
XLA Modules:
  0.0 34.5 jit_solution(16027094258081289206)
XLA Ops:
  0.0 33.8 %shard_map.109 = bf16[1024,128]{1,0:T(8,128)(2,1)S(1)} custom-call(bf16[1024,128]{1,0:T(8,128)(2,1)} %bitcast.5, bf16[4,8,128]{2,1,0:T(8,128)(2,1)} %diff_hbm.1, bf16[16,32,1024]{2,1,0:T(8,128)(2,1)} %bitcast.4, bf16[32,32]{1,0:T(8,128)(2,1)} %point_hbm.1, f32[32]{0:T(128)} %off_hbm.1, bf16[256,512]{1,0:T(8,128)(2,1)} %constant.21.tz_hbm, ...), custom_call_target="tpu_custom_call" | custom-call | tf_op jit(solution)/shard_map/pallas_call | solution.py:293
  33.8 0.7 %copy.13 = bf16[32,4,8,128]{3,2,1,0:T(8,128)(2,1)} copy(bf16[32,4,8,128]{3,2,1,0:T(8,128)(2,1)S(1)} %bitcast.3) | data formatting | bytes 524288

commit v5 on v4

--- a/solution.py
+++ b/solution.py
@@ -46,11 +46,12 @@
     co = np.einsum("hyHk,s,r->hyHksr", np.exp(-1j * ph), np.conj(unit), unit)
     ty = np.einsum("qhyHksr,cd->hrcysHkqd", parts(co), eye8).reshape(512, 512)
     x = 4 * (4 * np.arange(8)[None, :, None] + np.arange(4)[:, None, None]) + np.arange(4)
-    kx = freq(64).reshape(32, 2).T
-    th = turn(kx[None, None, None, :, :], x[:, :, :, None, None], 128)
+    kx = np.transpose(freq(64).reshape(4, 8, 2), (0, 2, 1))
+    th = turn(kx[None, None, None], x[:, :, :, None, None, None], 128)
     cs = np.stack([np.cos(th), np.sin(th)])
-    tx = np.einsum("sZYxlg,cd->ZlgcsYdx", cs, eye4).reshape(4, 256, 256)
-    txi = np.einsum("sZYxlg,cd->ZsYcxlgd", cs, eye4).reshape(4, 256, 256)
+    tx = np.einsum("sZYxylg,cd->ZylgcsYdx", cs, eye4).reshape(4, 4, 64, 256)
+    cs = cs.reshape(2, 4, 4, 2, 4, 4, 2, 8)
+    txi = np.einsum("sZYhxylg,cd->ZYshcxlygd", cs, eye4).reshape(4, 4, 64, 256)
     co = np.einsum("HyhK,s,r->HyhKsr", np.exp(1j * ph), unit, unit)
     tyi = np.einsum("qHyhKsr,bd->shbKrHqdy", parts(co), eye8).reshape(512, 512)
     b = np.exp(1j * turn(kz[:, None], z[None, :], 128)) * 2.0**-7.5
@@ -98,28 +99,39 @@
     return mix + jnp.concatenate(cols, axis=1) + shift
 
 
-def forward_xy(r1, tx, ty):
+def forward_y(r1, ty):
     r1 = r1.reshape(512, 128)
     d = jnp.concatenate([r1[h * 128 : h * 128 + 128] for h in range(4)], axis=1)
     e = mm(d, ty).astype(BF)
-    o = mm(tx, jnp.concatenate([e[:, :256], e[:, 256:]], axis=0))
+    return jnp.concatenate([e[:, :256], e[:, 256:]], axis=0)
+
+
+def forward_x(e, tx):
+    o = mm(jnp.concatenate(tx, axis=0), e)
     res = []
-    for h in range(4):
-        lanes = slice(h * 64, h * 64 + 64)
-        both = jnp.concatenate([o[:128, lanes], o[128:, lanes]], axis=1)
-        res.append(both.astype(BF).reshape(32, 4, 128))
+    for k in range(len(tx)):
+        lo, hi = o[k * 64 : k * 64 + 32], o[k * 64 + 32 : k * 64 + 64]
+        both = [jnp.concatenate([lo[:, h * 64 : h * 64 + 64], hi[:, h * 64 : h * 64 + 64]], axis=1) for h in range(4)]
+        res.append([b.astype(BF).reshape(8, 4, 128) for b in both])
     return res
 
 
-def own_modes(r2):
+def spread_table():
+    row, col = iota((256, 512), 0) % 128, iota((256, 512), 1)
+    return one_hot((row % 4 == col // 128) & (row // 4 == col % 32))
+
+
+def order_table():
+    row, col = iota((128, 128), 0), iota((128, 128), 1)
+    return one_hot((row % 4 == col // 32) & (row // 4 == col % 32))
+
+
+def own_modes(r2, spread):
     r2 = r2.reshape(512, 128).astype(F32)
     u = r2[:128] + r2[128:256] + r2[256:384] + r2[384:]
     hi = u.astype(BF)
     lo = (u - hi.astype(F32)).astype(BF)
-    row, col = iota((256, 512), 0), iota((256, 512), 1)
-    row = row % 128
-    rep = one_hot((row % 4 == col // 128) & (row // 4 == col % 32))
-    return mm(jnp.concatenate([hi, lo], axis=0), rep, TN) * (2.0**-9.5)
+    return mm(jnp.concatenate([hi, lo], axis=0), spread, TN) * (2.0**-9.5)
 
 
 def sum_rows(acc):
@@ -136,7 +148,7 @@
     return join(join(four[0], four[2], 2), join(four[1], four[3], 2), 1)
 
 
-def mix_modes(u, w):
+def mix_modes(u, w, order):
     blocks = []
     for l in range(2):
         acc = []
@@ -153,28 +165,33 @@
         y = sum_rows(acc)
         blocks += [y[:, b * 128 : b * 128 + 128] for b in range(8)]
     a = jnp.concatenate(blocks, axis=0).astype(BF)
-    row, col = iota((128, 128), 0), iota((128, 128), 1)
-    perm = one_hot((row % 4 == col // 32) & (row // 4 == col % 32))
-    return mm(perm, a, NT).astype(BF).reshape(32, 4, 128)
-
-
-def inverse_xy(r3, txi, tyi):
+    return mm(order, a, NT).astype(BF).reshape(32, 4, 128)
+
+
+def modes_by_kx(r3):
     r3 = r3.reshape(512, 128)
-    d = jnp.concatenate(
+    return jnp.concatenate(
         [
             jnp.concatenate([r3[h * 128 : h * 128 + 128, l * 64 : l * 64 + 64] for h in range(4)], axis=1)
             for l in range(2)
         ],
         axis=0,
     )
-    g = mm(txi, d).astype(BF)
-    o = mm(jnp.concatenate([g[:128], g[128:]], axis=1), tyi).astype(BF)
-    return [o[:, h * 128 : h * 128 + 128].reshape(8, 4, 4, 128) for h in range(4)]
+
+
+def inverse_xy(d, txi, tyi):
+    g = mm(jnp.concatenate(txi, axis=0), d).astype(BF)
+    g = [jnp.concatenate([g[k * 64 : k * 64 + 32], g[k * 64 + 32 : k * 64 + 64]], axis=1) for k in range(len(txi))]
+    o = mm(jnp.concatenate(g, axis=0), tyi).astype(BF)
+    return [
+        [o[k * 32 : k * 32 + 32, h * 128 : h * 128 + 128].reshape(2, 4, 4, 128) for h in range(4)]
+        for k in range(len(txi))
+    ]
 
 
 def inverse_z(r4, tzi):
     halves = [
-        jnp.concatenate([r4[o].reshape(128, 128)[:, r * 64 : r * 64 + 64] for o in range(4)], axis=1)
+        jnp.concatenate([r4[:, o].reshape(128, 128)[:, r * 64 : r * 64 + 64] for o in range(4)], axis=1)
         for r in range(2)
     ]
     res = mm(jnp.concatenate(halves, axis=0), tzi, TN)
@@ -197,17 +214,18 @@
 def kernel(
     x_hbm, diff_hbm, w_hbm, point_hbm, off_hbm, tz_hbm, tx_hbm, ty_hbm, txi_hbm, tyi_hbm, tzi_hbm,
     out_ref,
-    x_v, diff_v, w_v, wide_v, point_ref, off_ref, tz_v, tx_v, ty_v, txi_v, tyi_v, tzi_v, pre_v,
+    x_v, diff_v, w_v, wide_v, spread_v, order_v, point_ref, off_ref, tz_v, tx_v, ty_v, txi_v, tyi_v, tzi_v, pre_v,
     s1, r1, s2, r2, s3, r3, s4, r4, load_sem, send_sem, recv_sem,
 ):
     g, h = lax.axis_index("gx"), lax.axis_index("gy")
     plane, zz = g // 4, g % 4
     kz = plane * 4 + h
     yy, xc, core = g // 8, (plane % 2) * 2 + h // 2, h % 2
-    ys = [lax.rem(yy + k, 4) * 8 for k in range(4)]
+    ys = [lax.rem(yy + k, 4) for k in range(4)]
     zs = [lax.rem(zz + k, 4) for k in range(4)]
     xs = [lax.rem(xc + k, 4) for k in range(4)]
-    ups = [[ys[a] + xs[b] // 2 * 4 for b in range(4)] for a in range(4)]
+    xhs = [xs[b] // 2 for b in range(4)]
+    ups = [[ys[a] * 8 + xhs[b] * 4 for b in range(4)] for a in range(4)]
     gys = [[xs[b] % 2 * 2 + c for c in (core, 1 - core)] for b in range(4)]
     everyone = [(ups[a][b] + zs[c], gys[b][d]) for a, b, c, d in far_first((4, 4, 4))]
     planar = [(ups[a][b], gys[b][d]) for a, b, d in far_first((4, 4))]
@@ -248,19 +266,26 @@
     for up, gy in planar:
         send(s1.at[up + gy], r1.at[slot], 0, (up + zz, gy))
     r1[slot] = s1[kz]
+    spread_v[...] = spread_table()
+    order_v[...] = order_table()
     for m in range(16):
         wide_v[m] = w_v[m].astype(F32)
     wait(r1.at[pl.ds(0, 31)], recv_sem.at[0])
 
-    for k, block in enumerate(forward_xy(r1[...], tx_v[...], ty_v[...])):
-        s2[k] = block
+    e = forward_y(r1[...], ty_v[...])
     slot = zz * 32 + kz
-    for gx, gy in everyone:
-        send(s2.at[gy, gx], r2.at[slot], 1, (gx, gy))
-    r2[slot] = s2[h, g]
+    for near in ((2, 1), (3, 0)):
+        for k, blocks in zip(near, forward_x(e, [tx_v[ys[k]] for k in near])):
+            for j, block in enumerate(blocks):
+                s2[j, ys[k]] = block
+        for a, b, c, d in far_first((4, 4, 4)):
+            if a in near:
+                up, gy = xhs[b] * 4 + zs[c], gys[b][d]
+                send(s2.at[gy, ys[a], up], r2.at[slot], 1, (ys[a] * 8 + up, gy))
+    r2[slot] = s2[h, yy, g % 8]
     wait(r2.at[pl.ds(0, 127)], recv_sem.at[1])
 
-    s3[...] = mix_modes(own_modes(r2[...]), lambda m: wide_v[m])
+    s3[...] = mix_modes(own_modes(r2[...], spread_v[...]), lambda m: wide_v[m], order_v[...])
     slot = h * 32 + g
     for a, b, c, d in far_first((4, 4, 4)):
         up, gy = ups[a][b], gys[b][d]
@@ -268,11 +293,15 @@
     r3[slot] = s3[kz]
     wait(r3.at[pl.ds(0, 127)], recv_sem.at[2])
 
-    for k, block in enumerate(inverse_xy(r3[...], txi_v[...], tyi_v[...])):
-        s4[:, k] = block
-    for up, gy in planar:
-        send(s4.at[up // 4, gy], r4.at[:, kz], 3, (up + zz, gy))
-    r4[:, kz] = s4[plane, h]
+    modes = modes_by_kx(r3[...])
+    for near in ((2, 1), (3, 0)):
+        for k, blocks in zip(near, inverse_xy(modes, [txi_v[ys[k]] for k in near], tyi_v[...])):
+            for j, block in enumerate(blocks):
+                s4[ys[k], :, j] = block
+        for a, b, d in far_first((4, 4)):
+            if a in near:
+                send(s4.at[ys[a], xhs[b], gys[b][d]], r4.at[kz], 3, (ups[a][b] + zz, gys[b][d]))
+    r4[kz] = s4[yy, plane % 2, h]
     wait(r1.at[pl.ds(0, 31)], recv_sem.at[3])
 
     act = gelu(pre_v[...] + inverse_z(r4[...], tzi_v[...]))
@@ -296,13 +325,13 @@
         in_specs=[hbm] * 11,
         out_specs=vmem,
         scratch_shapes=[
-            v((1024, 128), BF), v((4, 8, 128), BF), v((16, 32, 1024), BF), v((16, 32, 1024), F32), v((32, 32), BF), pltpu.SMEM((32,), F32),
-            v((256, 512), BF), v((256, 256), BF), v((512, 512), BF),
-            v((256, 256), BF), v((512, 512), BF), v((256, 512), BF), v((256, 512), F32),
+            v((1024, 128), BF), v((4, 8, 128), BF), v((16, 32, 1024), BF), v((16, 32, 1024), F32), v((256, 512), BF), v((128, 128), BF), v((32, 32), BF), pltpu.SMEM((32,), F32),
+            v((256, 512), BF), v((4, 64, 256), BF), v((512, 512), BF),
+            v((4, 64, 256), BF), v((512, 512), BF), v((256, 512), BF), v((256, 512), F32),
             v((32, 4, 4, 128), BF), v((32, 4, 4, 128), BF),
-            v((4, 32, 4, 128), BF), v((128, 4, 128), BF),
+            v((4, 4, 8, 4, 128), BF), v((128, 4, 128), BF),
             v((32, 4, 128), BF), v((128, 4, 128), BF),
-            v((8, 4, 4, 4, 128), BF), v((4, 32, 4, 128), BF),
+            v((4, 2, 4, 4, 4, 128), BF), v((32, 4, 4, 128), BF),
             pltpu.SemaphoreType.DMA((11,)), pltpu.SemaphoreType.DMA((4,)), pltpu.SemaphoreType.DMA((4,)),
         ],
         compiler_params=pltpu.CompilerParams(

time: 34.6 us -> 34.6 us (level)
  no operation moved by 1% of the time
where the time goes in v5:
time: 34.6 us; the launch traced here: 34.5 us
  Pallas kernels  33.8 us (98%)
  local copies, waits for them, and re-layouts  0.71 us (2%)
    pallas_call x1, Pallas kernels, on_device(): pl.pallas_call(kernel, out_shape=jax.ShapeDtypeStruct((1024, 128), BF), i...  33.8 us
    unnamed x1, local copies, waits for them, and re-layouts  0.71 us

profile of v5, /device:TPU:1, one launch (start us, length us, event | category | flops | bytes accessed | tf_op | source)
XLA Modules:
  0.0 34.5 jit_solution(5078119736744689329)
XLA Ops:
  0.0 33.8 %shard_map.109 = bf16[1024,128]{1,0:T(8,128)(2,1)S(1)} custom-call(bf16[1024,128]{1,0:T(8,128)(2,1)} %bitcast.5, bf16[4,8,128]{2,1,0:T(8,128)(2,1)} %diff_hbm.1, bf16[16,32,1024]{2,1,0:T(8,128)(2,1)} %bitcast.4, bf16[32,32]{1,0:T(8,128)(2,1)} %point_hbm.1, f32[32]{0:T(128)} %off_hbm.1, bf16[256,512]{1,0:T(8,128)(2,1)} %constant.21.tz_hbm, ...), custom_call_target="tpu_custom_call" | custom-call | tf_op jit(solution)/shard_map/pallas_call | solution.py:322
  33.8 0.7 %copy.13 = bf16[32,4,8,128]{3,2,1,0:T(8,128)(2,1)} copy(bf16[32,4,8,128]{3,2,1,0:T(8,128)(2,1)S(1)} %bitcast.3) | data formatting | bytes 524288

commit v6 on v5

--- a/solution.py
+++ b/solution.py
@@ -2,6 +2,7 @@
 
 import jax
 import jax.numpy as jnp
+import ml_dtypes
 import numpy as np
 from jax import lax
 from jax.experimental import pallas as pl
@@ -32,6 +33,11 @@
 
 def parts(z):
     return np.stack([z.real, z.imag])
+
+
+def two_parts(t, axis, order):
+    high = np.asarray(t, np.float32).astype(ml_dtypes.bfloat16).astype(np.float64)
+    return np.concatenate([(high, t - high)[k] for k in order], axis=axis)
 
 
 def tables():
@@ -56,7 +62,9 @@
     tyi = np.einsum("qHyhKsr,bd->shbKrHqdy", parts(co), eye8).reshape(512, 512)
     b = np.exp(1j * turn(kz[:, None], z[None, :], 128)) * 2.0**-7.5
     tzi = np.einsum("rkz,xw->rkxwz", np.stack([b.real, -b.imag]), eye4).reshape(256, 512)
-    return [jnp.asarray(np.asarray(t, np.float32)).astype(BF) for t in (tz, tx, ty, txi, tyi, tzi)]
+    tx, txi = two_parts(tx, 3, (0, 1, 0)), two_parts(txi, 3, (0, 1))
+    tzi = two_parts(tzi, 0, (0, 1))
+    return [jnp.asarray(np.asarray(t, np.float32).astype(ml_dtypes.bfloat16)) for t in (tz, tx, ty, txi, tyi, tzi)]
 
 
 def iota(shape, dim):
@@ -102,8 +110,10 @@
 def forward_y(r1, ty):
     r1 = r1.reshape(512, 128)
     d = jnp.concatenate([r1[h * 128 : h * 128 + 128] for h in range(4)], axis=1)
-    e = mm(d, ty).astype(BF)
-    return jnp.concatenate([e[:, :256], e[:, 256:]], axis=0)
+    e = mm(d, ty)
+    e = jnp.concatenate([e[:, :256], e[:, 256:]], axis=0)
+    high = e.astype(BF)
+    return jnp.concatenate([high, high, (e - high.astype(F32)).astype(BF)], axis=0)
 
 
 def forward_x(e, tx):
@@ -170,13 +180,14 @@
 
 def modes_by_kx(r3):
     r3 = r3.reshape(512, 128)
-    return jnp.concatenate(
+    d = jnp.concatenate(
         [
             jnp.concatenate([r3[h * 128 : h * 128 + 128, l * 64 : l * 64 + 64] for h in range(4)], axis=1)
             for l in range(2)
         ],
         axis=0,
     )
+    return jnp.concatenate([d, d], axis=0)
 
 
 def inverse_xy(d, txi, tyi):
@@ -194,7 +205,7 @@
         jnp.concatenate([r4[:, o].reshape(128, 128)[:, r * 64 : r * 64 + 64] for o in range(4)], axis=1)
         for r in range(2)
     ]
-    res = mm(jnp.concatenate(halves, axis=0), tzi, TN)
+    res = mm(jnp.concatenate(halves + halves, axis=0), tzi, TN)
     return jnp.transpose(res.reshape(4, 8, 8, 512), (1, 0, 2, 3)).reshape(256, 512)
 
 
@@ -326,8 +337,8 @@
         out_specs=vmem,
         scratch_shapes=[
             v((1024, 128), BF), v((4, 8, 128), BF), v((16, 32, 1024), BF), v((16, 32, 1024), F32), v((256, 512), BF), v((128, 128), BF), v((32, 32), BF), pltpu.SMEM((32,), F32),
-            v((256, 512), BF), v((4, 64, 256), BF), v((512, 512), BF),
-            v((4, 64, 256), BF), v((512, 512), BF), v((256, 512), BF), v((256, 512), F32),
+            v((256, 512), BF), v((4, 64, 768), BF), v((512, 512), BF),
+            v((4, 64, 512), BF), v((512, 512), BF), v((512, 512), BF), v((256, 512), F32),
             v((32, 4, 4, 128), BF), v((32, 4, 4, 128), BF),
             v((4, 4, 8, 4, 128), BF), v((128, 4, 128), BF),
             v((32, 4, 128), BF), v((128, 4, 128), BF),

time: 34.6 us -> 34.9 us (level)
  no operation moved by 1% of the time
where the time goes in v6:
time: 34.9 us; the launch traced here: 34.7 us
  Pallas kernels  34 us (97%)
  local copies, waits for them, and re-layouts  0.71 us (2%)
    pallas_call x1, Pallas kernels, on_device(): pl.pallas_call(kernel, out_shape=jax.ShapeDtypeStruct((1024, 128), BF), i...  34 us
    unnamed x1, local copies, waits for them, and re-layouts  0.71 us

profile of v6, /device:TPU:1, one launch (start us, length us, event | category | flops | bytes accessed | tf_op | source)
XLA Modules:
  0.0 34.7 jit_solution(16734472426285070532)
XLA Ops:
  0.0 34.0 %shard_map.109 = bf16[1024,128]{1,0:T(8,128)(2,1)S(1)} custom-call(bf16[1024,128]{1,0:T(8,128)(2,1)} %bitcast.5, bf16[4,8,128]{2,1,0:T(8,128)(2,1)} %diff_hbm.1, bf16[16,32,1024]{2,1,0:T(8,128)(2,1)} %bitcast.4, bf16[32,32]{1,0:T(8,128)(2,1)} %point_hbm.1, f32[32]{0:T(128)} %off_hbm.1, bf16[256,512]{1,0:T(8,128)(2,1)} %constant.12.clone.tz_hbm, ...), custom_call_target="tpu_custom_call" | custom-call | tf_op jit(solution)/shard_map/pallas_call | solution.py:333
  34.0 0.7 %copy.13 = bf16[32,4,8,128]{3,2,1,0:T(8,128)(2,1)} copy(bf16[32,4,8,128]{3,2,1,0:T(8,128)(2,1)S(1)} %bitcast.3) | data formatting | bytes 524288

commit v7 on v6

--- a/solution.py
+++ b/solution.py
@@ -158,20 +158,20 @@
     return join(join(four[0], four[2], 2), join(four[1], four[3], 2), 1)
 
 
-def mix_modes(u, w, order):
+def mix_modes(u, w, both, order):
     blocks = []
     for l in range(2):
         acc = []
         for j in range(4 * l, 4 * l + 4):
-            wr, wi = w(2 * j), w(2 * j + 1)
-            re = im = None
+            wr, wi, ws = w(2 * j), w(2 * j + 1), both(j)
+            total = None
             for q in range(4):
                 ur = jnp.concatenate([u[16 * j : 16 * j + 8, q * 128 : q * 128 + 128]] * 8, axis=1)
                 ui = jnp.concatenate([u[16 * j + 8 : 16 * j + 16, q * 128 : q * 128 + 128]] * 8, axis=1)
                 r, i = wr[q * 8 : q * 8 + 8], wi[q * 8 : q * 8 + 8]
-                a, b = r * ur - i * ui, r * ui + i * ur
-                re, im = (a, b) if re is None else (re + a, im + b)
-            acc += [re, im]
+                p = ws[q * 8 : q * 8 + 8] * ur, r * (ui - ur), i * (ur + ui)
+                total = p if total is None else [a + b for a, b in zip(total, p)]
+            acc += [total[0] - total[2], total[0] + total[1]]
         y = sum_rows(acc)
         blocks += [y[:, b * 128 : b * 128 + 128] for b in range(8)]
     a = jnp.concatenate(blocks, axis=0).astype(BF)
@@ -225,7 +225,7 @@
 def kernel(
     x_hbm, diff_hbm, w_hbm, point_hbm, off_hbm, tz_hbm, tx_hbm, ty_hbm, txi_hbm, tyi_hbm, tzi_hbm,
     out_ref,
-    x_v, diff_v, w_v, wide_v, spread_v, order_v, point_ref, off_ref, tz_v, tx_v, ty_v, txi_v, tyi_v, tzi_v, pre_v,
+    x_v, diff_v, w_v, wide_v, both_v, spread_v, order_v, point_ref, off_ref, tz_v, tx_v, ty_v, txi_v, tyi_v, tzi_v, pre_v,
     s1, r1, s2, r2, s3, r3, s4, r4, load_sem, send_sem, recv_sem,
 ):
     g, h = lax.axis_index("gx"), lax.axis_index("gy")
@@ -281,6 +281,8 @@
     order_v[...] = order_table()
     for m in range(16):
         wide_v[m] = w_v[m].astype(F32)
+    for j in range(8):
+        both_v[j] = wide_v[2 * j] + wide_v[2 * j + 1]
     wait(r1.at[pl.ds(0, 31)], recv_sem.at[0])
 
     e = forward_y(r1[...], ty_v[...])
@@ -296,7 +298,7 @@
     r2[slot] = s2[h, yy, g % 8]
     wait(r2.at[pl.ds(0, 127)], recv_sem.at[1])
 
-    s3[...] = mix_modes(own_modes(r2[...], spread_v[...]), lambda m: wide_v[m], order_v[...])
+    s3[...] = mix_modes(own_modes(r2[...], spread_v[...]), lambda m: wide_v[m], lambda j: both_v[j], order_v[...])
     slot = h * 32 + g
     for a, b, c, d in far_first((4, 4, 4)):
         up, gy = ups[a][b], gys[b][d]
@@ -336,7 +338,7 @@
         in_specs=[hbm] * 11,
         out_specs=vmem,
         scratch_shapes=[
-            v((1024, 128), BF), v((4, 8, 128), BF), v((16, 32, 1024), BF), v((16, 32, 1024), F32), v((256, 512), BF), v((128, 128), BF), v((32, 32), BF), pltpu.SMEM((32,), F32),
+            v((1024, 128), BF), v((4, 8, 128), BF), v((16, 32, 1024), BF), v((16, 32, 1024), F32), v((8, 32, 1024), F32), v((256, 512), BF), v((128, 128), BF), v((32, 32), BF), pltpu.SMEM((32,), F32),
             v((256, 512), BF), v((4, 64, 768), BF), v((512, 512), BF),
             v((4, 64, 512), BF), v((512, 512), BF), v((512, 512), BF), v((256, 512), F32),
             v((32, 4, 4, 128), BF), v((32, 4, 4, 128), BF),

time: 34.9 us -> 34.7 us (level)
  no operation moved by 1% of the time
where the time goes in v7:
time: 34.7 us; the launch traced here: 34.6 us
  Pallas kernels  33.9 us (98%)
  local copies, waits for them, and re-layouts  0.71 us (2%)
    pallas_call x1, Pallas kernels, on_device(): pl.pallas_call(kernel, out_shape=jax.ShapeDtypeStruct((1024, 128), BF), i...  33.9 us
    unnamed x1, local copies, waits for them, and re-layouts  0.71 us

profile of v7, /device:TPU:1, one launch (start us, length us, event | category | flops | bytes accessed | tf_op | source)
XLA Modules:
  0.0 34.6 jit_solution(461359597985608151)
XLA Ops:
  0.0 33.9 %shard_map.109 = bf16[1024,128]{1,0:T(8,128)(2,1)S(1)} custom-call(bf16[1024,128]{1,0:T(8,128)(2,1)} %bitcast.5, bf16[4,8,128]{2,1,0:T(8,128)(2,1)} %diff_hbm.1, bf16[16,32,1024]{2,1,0:T(8,128)(2,1)} %bitcast.4, bf16[32,32]{1,0:T(8,128)(2,1)} %point_hbm.1, f32[32]{0:T(128)} %off_hbm.1, bf16[256,512]{1,0:T(8,128)(2,1)} %constant.12.clone.tz_hbm, ...), custom_call_target="tpu_custom_call" | custom-call | tf_op jit(solution)/shard_map/pallas_call | solution.py:335
  33.9 0.7 %copy.13 = bf16[32,4,8,128]{3,2,1,0:T(8,128)(2,1)} copy(bf16[32,4,8,128]{3,2,1,0:T(8,128)(2,1)S(1)} %bitcast.3) | data formatting | bytes 524288

commit v8 on v6

--- a/solution.py
+++ b/solution.py
@@ -285,7 +285,7 @@
 
     e = forward_y(r1[...], ty_v[...])
     slot = zz * 32 + kz
-    for near in ((2, 1), (3, 0)):
+    for near in ((2, 1, 3, 0),):
         for k, blocks in zip(near, forward_x(e, [tx_v[ys[k]] for k in near])):
             for j, block in enumerate(blocks):
                 s2[j, ys[k]] = block
@@ -305,7 +305,7 @@
     wait(r3.at[pl.ds(0, 127)], recv_sem.at[2])
 
     modes = modes_by_kx(r3[...])
-    for near in ((2, 1), (3, 0)):
+    for near in ((2, 1, 3, 0),):
         for k, blocks in zip(near, inverse_xy(modes, [txi_v[ys[k]] for k in near], tyi_v[...])):
             for j, block in enumerate(blocks):
                 s4[ys[k], :, j] = block

time: 34.9 us -> 34.9 us (level)
  no operation moved by 1% of the time
where the time goes in v8:
time: 34.9 us; the launch traced here: 34.8 us
  Pallas kernels  34.1 us (98%)
  local copies, waits for them, and re-layouts  0.71 us (2%)
    pallas_call x1, Pallas kernels, on_device(): pl.pallas_call(kernel, out_shape=jax.ShapeDtypeStruct((1024, 128), BF), i...  34.1 us
    unnamed x1, local copies, waits for them, and re-layouts  0.71 us

profile of v8, /device:TPU:1, one launch (start us, length us, event | category | flops | bytes accessed | tf_op | source)
XLA Modules:
  0.0 34.8 jit_solution(3678236035796060468)
XLA Ops:
  0.0 34.1 %shard_map.109 = bf16[1024,128]{1,0:T(8,128)(2,1)S(1)} custom-call(bf16[1024,128]{1,0:T(8,128)(2,1)} %bitcast.5, bf16[4,8,128]{2,1,0:T(8,128)(2,1)} %diff_hbm.1, bf16[16,32,1024]{2,1,0:T(8,128)(2,1)} %bitcast.4, bf16[32,32]{1,0:T(8,128)(2,1)} %point_hbm.1, f32[32]{0:T(128)} %off_hbm.1, bf16[256,512]{1,0:T(8,128)(2,1)} %constant.12.clone.tz_hbm, ...), custom_call_target="tpu_custom_call" | custom-call | tf_op jit(solution)/shard_map/pallas_call | solution.py:333
  34.1 0.7 %copy.13 = bf16[32,4,8,128]{3,2,1,0:T(8,128)(2,1)} copy(bf16[32,4,8,128]{3,2,1,0:T(8,128)(2,1)S(1)} %bitcast.3) | data formatting | bytes 524288

commit v9 on v6

--- a/solution.py
+++ b/solution.py
@@ -63,7 +63,6 @@
     b = np.exp(1j * turn(kz[:, None], z[None, :], 128)) * 2.0**-7.5
     tzi = np.einsum("rkz,xw->rkxwz", np.stack([b.real, -b.imag]), eye4).reshape(256, 512)
     tx, txi = two_parts(tx, 3, (0, 1, 0)), two_parts(txi, 3, (0, 1))
-    tzi = two_parts(tzi, 0, (0, 1))
     return [jnp.asarray(np.asarray(t, np.float32).astype(ml_dtypes.bfloat16)) for t in (tz, tx, ty, txi, tyi, tzi)]
 
 
@@ -205,7 +204,7 @@
         jnp.concatenate([r4[:, o].reshape(128, 128)[:, r * 64 : r * 64 + 64] for o in range(4)], axis=1)
         for r in range(2)
     ]
-    res = mm(jnp.concatenate(halves + halves, axis=0), tzi, TN)
+    res = mm(jnp.concatenate(halves, axis=0), tzi, TN)
     return jnp.transpose(res.reshape(4, 8, 8, 512), (1, 0, 2, 3)).reshape(256, 512)
 
 
@@ -338,7 +337,7 @@
         scratch_shapes=[
             v((1024, 128), BF), v((4, 8, 128), BF), v((16, 32, 1024), BF), v((16, 32, 1024), F32), v((256, 512), BF), v((128, 128), BF), v((32, 32), BF), pltpu.SMEM((32,), F32),
             v((256, 512), BF), v((4, 64, 768), BF), v((512, 512), BF),
-            v((4, 64, 512), BF), v((512, 512), BF), v((512, 512), BF), v((256, 512), F32),
+            v((4, 64, 512), BF), v((512, 512), BF), v((256, 512), BF), v((256, 512), F32),
             v((32, 4, 4, 128), BF), v((32, 4, 4, 128), BF),
             v((4, 4, 8, 4, 128), BF), v((128, 4, 128), BF),
             v((32, 4, 128), BF), v((128, 4, 128), BF),

time: 34.9 us -> 34.8 us (level)
  no operation moved by 1% of the time
where the time goes in v9:
time: 34.8 us; the launch traced here: 34.7 us
  Pallas kernels  34 us (98%)
  local copies, waits for them, and re-layouts  0.71 us (2%)
    pallas_call x1, Pallas kernels, on_device(): pl.pallas_call(kernel, out_shape=jax.ShapeDtypeStruct((1024, 128), BF), i...  34 us
    unnamed x1, local copies, waits for them, and re-layouts  0.71 us

profile of v9, /device:TPU:1, one launch (start us, length us, event | category | flops | bytes accessed | tf_op | source)
XLA Modules:
  0.0 34.7 jit_solution(13979539832842587025)
XLA Ops:
  0.0 34.0 %shard_map.109 = bf16[1024,128]{1,0:T(8,128)(2,1)S(1)} custom-call(bf16[1024,128]{1,0:T(8,128)(2,1)} %bitcast.5, bf16[4,8,128]{2,1,0:T(8,128)(2,1)} %diff_hbm.1, bf16[16,32,1024]{2,1,0:T(8,128)(2,1)} %bitcast.4, bf16[32,32]{1,0:T(8,128)(2,1)} %point_hbm.1, f32[32]{0:T(128)} %off_hbm.1, bf16[256,512]{1,0:T(8,128)(2,1)} %constant.12.clone.tz_hbm, ...), custom_call_target="tpu_custom_call" | custom-call | tf_op jit(solution)/shard_map/pallas_call | solution.py:332
  34.0 0.7 %copy.13 = bf16[32,4,8,128]{3,2,1,0:T(8,128)(2,1)} copy(bf16[32,4,8,128]{3,2,1,0:T(8,128)(2,1)S(1)} %bitcast.3) | data formatting | bytes 524288

commit v10 on v9

--- a/solution.py
+++ b/solution.py
@@ -304,13 +304,15 @@
     wait(r3.at[pl.ds(0, 127)], recv_sem.at[2])
 
     modes = modes_by_kx(r3[...])
-    for near in ((2, 1), (3, 0)):
-        for k, blocks in zip(near, inverse_xy(modes, [txi_v[ys[k]] for k in near], tyi_v[...])):
-            for j, block in enumerate(blocks):
-                s4[ys[k], :, j] = block
-        for a, b, d in far_first((4, 4)):
-            if a in near:
-                send(s4.at[ys[a], xhs[b], gys[b][d]], r4.at[kz], 3, (ups[a][b] + zz, gys[b][d]))
+    for k, blocks in enumerate(inverse_xy(modes, [txi_v[k] for k in range(4)], tyi_v[...])):
+        for j, block in enumerate(blocks):
+            s4[k, :, j] = block
+    places = [(p, q, c) for p in range(4) for q in range(4) for c in range(2)]
+    for yd, xd, cd in sorted(places, key=lambda t: (t[0] + t[1], t)):
+
+        @pl.when((yy != yd) | (xc != xd) | (core != cd))
+        def _(yd=yd, xh=xd // 2, gy=xd % 2 * 2 + cd):
+            send(s4.at[yd, xh, gy], r4.at[kz], 3, (yd * 8 + xh * 4 + zz, gy))
     r4[kz] = s4[yy, plane % 2, h]
     wait(r1.at[pl.ds(0, 31)], recv_sem.at[3])
 

time: 34.8 us -> 34.7 us (level)
  no operation moved by 1% of the time
where the time goes in v10:
time: 34.7 us; the launch traced here: 34.6 us
  Pallas kernels  33.9 us (98%)
  local copies, waits for them, and re-layouts  0.71 us (2%)
    pallas_call x1, Pallas kernels, on_device(): pl.pallas_call(kernel, out_shape=jax.ShapeDtypeStruct((1024, 128), BF), i...  33.9 us
    unnamed x1, local copies, waits for them, and re-layouts  0.71 us

profile of v10, /device:TPU:1, one launch (start us, length us, event | category | flops | bytes accessed | tf_op | source)
XLA Modules:
  0.0 34.6 jit_solution(1732597495511901129)
XLA Ops:
  0.0 33.9 %shard_map.109 = bf16[1024,128]{1,0:T(8,128)(2,1)S(1)} custom-call(bf16[1024,128]{1,0:T(8,128)(2,1)} %bitcast.5, bf16[4,8,128]{2,1,0:T(8,128)(2,1)} %diff_hbm.1, bf16[16,32,1024]{2,1,0:T(8,128)(2,1)} %bitcast.4, bf16[32,32]{1,0:T(8,128)(2,1)} %point_hbm.1, f32[32]{0:T(128)} %off_hbm.1, bf16[256,512]{1,0:T(8,128)(2,1)} %constant.12.clone.tz_hbm, ...), custom_call_target="tpu_custom_call" | custom-call | tf_op jit(solution)/shard_map/pallas_call | solution.py:334
  33.9 0.7 %copy.13 = bf16[32,4,8,128]{3,2,1,0:T(8,128)(2,1)} copy(bf16[32,4,8,128]{3,2,1,0:T(8,128)(2,1)S(1)} %bitcast.3) | data formatting | bytes 524288
